TPU v7x, 128 devices: a whole 4x4x4 slice. The times are simulated.
128 devices in a mesh: src: 4 (over y), seq: 32 (over x, z, core).
Axes of the slice: x: 4, y: 4, z: 4, core: 2. Of those that a mesh axis runs over, the one named last changes fastest.
Arguments:
- kv_delta: bfloat16 [16, 32, 32, 16, 2048], P('src', None, 'seq'), may hold values from -6 to 6
- anchors: bfloat16 [16, 32, 32, 2048], P('src', None, 'seq'), may hold values from -6 to 6
- scales: float32 [16, 32, 32, 16], P('src', None, 'seq'), may hold values from 0.1 to 1
- in_len: int32 [16], replicated, may hold values from 1 to 16384, 131072 in all
- assign: int32 [16], replicated, may hold values from 0 to 15, as said below
- res_cache: bfloat16 [16, 8192, 2048], P('src', 'seq'), may hold values from -6 to 6
- res_len: int32 [16], replicated, may hold values from 1 to 8192, 65536 in all
- queries: bfloat16 [32, 4, 8192], P('src'), may hold values from -110 to 110
- fresh_key_value: bfloat16 [32, 4, 2048], P('src'), may hold values from -6 to 6
Outputs:
- in_cache: bfloat16 [16, 16384, 2048], P('src', 'seq')
- attention: bfloat16 [32, 4, 8192], P('src')
Inputs may be any that keep to these rules, and one draw needn't show every extreme that they name: `assign`: a permutation of the incoming slots; decode replica p holds slots p * 4 to (p + 1) * 4 - 1 and receives exactly 1 request from each prefill replica.
All inputs are finite; a program needn't handle non-finite values.
Results may differ from a plain program's by a relative error of at most 0.012.
The roundings to bfloat16 on the way count: a program that leaves them out, or rounds other values in their place, can miss the bound.
Values may be sent and summed in bfloat16 or wider, within the bound.
A program may use at most 192 MiB of HBM per device.

v0:
```python
import math

import jax
import jax.numpy as jnp
from jax import lax
from jax.sharding import PartitionSpec as P

QUERY_HEADS = 64
KEY_VALUE_HEADS = 8
HEAD_SIZE = 128


def combined_all(part, axis, combine):
    gathered = jax.tree.map(lambda a: lax.all_gather(a, axis), part)

    def take(source):
        return jax.tree.map(lambda a: lax.dynamic_index_in_dim(a, source, 0, False), gathered)

    return lax.fori_loop(
        1, lax.axis_size(axis), lambda source, state: combine(state, take(source)), take(0)
    )


def partial_state(query_row_list, cached_row_list, valid_mask):
    decode_slot_count = query_row_list.shape[0]
    decode_step_count = query_row_list.shape[1]
    key_span_width = KEY_VALUE_HEADS * HEAD_SIZE
    query_head_list = query_row_list.reshape(
        decode_slot_count,
        decode_step_count,
        KEY_VALUE_HEADS,
        QUERY_HEADS // KEY_VALUE_HEADS,
        HEAD_SIZE,
    )
    key_row_list = cached_row_list[:, :, :key_span_width].reshape(
        decode_slot_count, -1, KEY_VALUE_HEADS, HEAD_SIZE
    )
    value_row_list = cached_row_list[:, :, key_span_width:].reshape(
        decode_slot_count, -1, KEY_VALUE_HEADS, HEAD_SIZE
    )
    scores = jnp.einsum(
        "nshgd,nthd->nhsgt", query_head_list, key_row_list, preferred_element_type=jnp.float32
    ) / math.sqrt(HEAD_SIZE)
    keep_mask = valid_mask[:, None, None, None, :]
    scores = jnp.where(keep_mask, scores, -1e30)
    row_peak = jnp.max(scores, axis=-1)
    weights = jnp.where(keep_mask, jnp.exp(scores - row_peak[..., None]), 0.0)
    row_total = jnp.sum(weights, axis=-1)
    summed = jnp.einsum(
        "nhsgt,nthd->nhsgd",
        weights.astype(jnp.bfloat16),
        value_row_list,
        preferred_element_type=jnp.float32,
    )
    return (row_peak, row_total, summed)


def combine_states(left_state, right_state):
    left_peak, left_total, left_sum = left_state
    right_peak, right_total, right_sum = right_state
    row_peak = jnp.maximum(left_peak, right_peak)
    left_factor = jnp.exp(left_peak - row_peak)
    right_factor = jnp.exp(right_peak - row_peak)
    row_total = left_total * left_factor + right_total * right_factor
    summed = left_sum * left_factor[..., None] + right_sum * right_factor[..., None]
    return (row_peak, row_total, summed)


def on_device(
    kv_delta, anchors, scales, in_len, assign, res_cache, res_len, queries, fresh_key_value
):
    src_count = lax.axis_size("src")
    seq_count = lax.axis_size("seq")
    src_index = lax.axis_index("src")
    seq_index = lax.axis_index("seq")
    local_reqs = kv_delta.shape[0]
    per_pair = local_reqs // src_count
    group_len = kv_delta.shape[3]
    feature = kv_delta.shape[4]
    own_slots = lax.dynamic_slice_in_dim(assign, src_index * local_reqs, local_reqs)
    send_order = jnp.argsort(own_slots)
    scale_wide = jnp.repeat(scales, HEAD_SIZE, axis=-1)
    restored_cache = (
        anchors.astype(jnp.float32)[:, :, :, None, :]
        + scale_wide[:, :, :, None, :] * kv_delta.astype(jnp.float32)
    ).astype(jnp.bfloat16)
    ordered = jnp.take(restored_cache, send_order, axis=0).reshape(
        src_count, per_pair, seq_count, 1, group_len, feature
    )
    sorted_slots = jnp.sort(assign.reshape(src_count, local_reqs), axis=1)
    arrived = (
        lax.dynamic_slice_in_dim(sorted_slots, src_index * per_pair, per_pair, 1)
        - src_index * local_reqs
    )
    local_ids = jnp.arange(local_reqs)
    matches = (arrived[None, :, :] == local_ids[:, None, None]).astype(jnp.int32)
    from_src = jnp.sum(matches * jnp.arange(src_count)[None, :, None], axis=(1, 2))
    from_pair = jnp.sum(matches * jnp.arange(per_pair)[None, None, :], axis=(1, 2))
    flat_rows = ordered.transpose(0, 2, 1, 3, 4, 5).reshape(
        src_count * seq_count, per_pair, 1, group_len, feature
    )
    moved_rows = lax.all_to_all(flat_rows, ("src", "seq"), split_axis=0, concat_axis=2, tiled=True)
    pieces = moved_rows.reshape(per_pair, src_count, seq_count * group_len, feature)
    in_cache = pieces[from_pair, from_src]
    slot_ids = src_index * local_reqs + local_ids
    slot_len = jnp.sum(jnp.where(assign[:, None] == slot_ids[None, :], in_len[:, None], 0), axis=0)
    span_in = in_cache.shape[1]
    in_valid = (seq_index * span_in + jnp.arange(span_in))[None, :] < slot_len[:, None]
    in_cache = jnp.where(in_valid[:, :, None], in_cache, jnp.zeros_like(in_cache))
    res_count = res_cache.shape[0]
    res_own = lax.dynamic_slice_in_dim(res_len, src_index * res_count, res_count)
    span_res = res_cache.shape[1]
    res_valid = (seq_index * span_res + jnp.arange(span_res))[None, :] < res_own[:, None]
    in_peak, in_total, in_sum = partial_state(queries[:local_reqs], in_cache, in_valid)
    res_peak, res_total, res_sum = partial_state(queries[local_reqs:], res_cache, res_valid)
    joined = (
        jnp.concatenate([in_peak, res_peak], axis=0),
        jnp.concatenate([in_total, res_total], axis=0),
        jnp.concatenate([in_sum, res_sum], axis=0),
    )
    row_peak, row_total, summed = combined_all(joined, "seq", combine_states)
    decode_slot_count = queries.shape[0]
    decode_step_count = queries.shape[1]
    key_span_width = KEY_VALUE_HEADS * HEAD_SIZE
    query_head_list = queries.reshape(
        decode_slot_count,
        decode_step_count,
        KEY_VALUE_HEADS,
        QUERY_HEADS // KEY_VALUE_HEADS,
        HEAD_SIZE,
    )
    fresh_keys = fresh_key_value[:, :, :key_span_width].reshape(
        decode_slot_count, decode_step_count, KEY_VALUE_HEADS, HEAD_SIZE
    )
    fresh_values = fresh_key_value[:, :, key_span_width:].reshape(
        decode_slot_count, decode_step_count, KEY_VALUE_HEADS, HEAD_SIZE
    )
    new_scores = jnp.einsum(
        "nshgd,nthd->nhsgt", query_head_list, fresh_keys, preferred_element_type=jnp.float32
    ) / math.sqrt(HEAD_SIZE)
    causal = (jnp.arange(decode_step_count)[None, :] <= jnp.arange(decode_step_count)[:, None])[
        None, None, :, None, :
    ]
    new_scores = jnp.where(causal, new_scores, -1e30)
    top_score = jnp.maximum(row_peak, jnp.max(new_scores, axis=-1))
    old_factor = jnp.exp(row_peak - top_score)
    new_weights = jnp.where(causal, jnp.exp(new_scores - top_score[..., None]), 0.0)
    row_total = row_total * old_factor + jnp.sum(new_weights, axis=-1)
    summed = summed * old_factor[..., None] + jnp.einsum(
        "nhsgt,nthd->nhsgd",
        new_weights.astype(jnp.bfloat16),
        fresh_values,
        preferred_element_type=jnp.float32,
    )
    result = (
        (summed / row_total[..., None])
        .transpose(0, 2, 1, 3, 4)
        .reshape(decode_slot_count, decode_step_count, QUERY_HEADS * HEAD_SIZE)
    )
    return (in_cache, result.astype(jnp.bfloat16))


def solution(mesh):
    in_specs = (
        P("src", None, "seq", None, None),
        P("src", None, "seq", None),
        P("src", None, "seq", None),
        P(),
        P(),
        P("src", "seq", None),
        P(),
        P("src", None, None),
        P("src", None, None),
    )
    out_specs = (P("src", "seq", None), P("src", None, None))
    return jax.shard_map(
        on_device, mesh=mesh, in_specs=in_specs, out_specs=out_specs, check_vma=False
    )
```

profile of v0, /device:TPU:1, one launch (start us, length us, event | category | flops | bytes accessed | tf_op | source)
XLA Modules:
  0.0 445.3 jit_solution(16188667478464413220)
XLA Ops:
  11.2 5.5 %add_convert_fusion = bf16[4,32,1,16,2048]{4,3,2,1,0:T(8,128)(2,1)S(1)} fusion(bf16[4,32,1,16,2048]{4,3,2,1,0:T(8,128)(2,1)} %param.11, f32[4,32,2048]{2,1,0:T(8,128)S(1)} %broadcast_in_dim.139, f32[4,32,2048]{2,1,0:T(8,128)S(1)} %bitcast_convert_fusion), kind=kLoop, calls=%fused_computation.15 | loop fusion | flops 16777216 | bytes 18874368 | tf_op jit(solution)/shard_map/convert_element_type | solution.py:86
  16.7 3.8 slice_bitcast_fusion.1
  20.5 5.0 %gather_fusion = bf16[4,32,16,1024]{3,2,1,0:T(8,128)(2,1)} fusion(bf16[4,32,16,1024]{3,2,1,0:T(8,128)(2,1)} %get-tuple-element.243, s32[1024]{0:T(1024)S(1)} %pad_clamp_fusion), kind=kCustom, calls=%fused_computation | custom fusion | bytes 8388624 | tf_op jit(solution)/shard_map/jit(_take)/gather | solution.py:87
  25.5 5.0 %gather_fusion.1 = bf16[4,32,16,1024]{3,2,1,0:T(8,128)(2,1)} fusion(bf16[4,32,16,1024]{3,2,1,0:T(8,128)(2,1)} %get-tuple-element.244, s32[1024]{0:T(1024)S(1)} %pad_clamp_fusion), kind=kCustom, calls=%fused_computation.1 | custom fusion | bytes 8388624 | tf_op jit(solution)/shard_map/jit(_take)/gather | solution.py:87
  30.6 8.4 %pad_maximum_fusion = bf16[4,32,1,16,2048]{4,3,1,0,2:T(8,128)(2,1)} fusion(bf16[4,32,1,16,1024]{4,3,1,0,2:T(8,128)(2,1)} %bitcast.110, bf16[4,32,1,16,1024]{4,3,1,0,2:T(8,128)(2,1)} %bitcast.109), kind=kLoop, calls=%fused_computation.16 | loop fusion | flops 16777216 | bytes 16777216
  39.0 7.4 %bitcast_select_fusion = bf16[128,1,1,16,2048]{4,3,2,1,0:T(8,128)(2,1)} fusion(bf16[4,32,1,16,2048]{4,3,1,0,2:T(8,128)(2,1)} %pad_maximum_fusion, pred[128]{0:T(512)(128)(4,1)S(1)} %broadcast_in_dim.136), kind=kLoop, calls=%fused_computation.18 | loop fusion | flops 4194304 | bytes 16777344 | tf_op jit(solution)/shard_map/jit(_take)/select_n | solution.py:87
  46.4 12.0 %all-to-all-start = ((bf16[128,1,1,16,2048]{4,3,2,1,0:T(8,128)(2,1)}), bf16[128,1,1,16,2048]{4,3,2,1,0:T(8,128)(2,1)}, u32[]{:S(2)}, u32[]{:S(2)}) async-start(bf16[128,1,1,16,2048]{4,3,2,1,0:T(8,128)(2,1)} %bitcast_select_fusion), calls=%async_computation | async-start | bytes 16777216 | tf_op jit(solution)/shard_map/all_to_all | solution.py:102
  60.0 4.7 %fusion.53 = (bf16[4,256,1024]{2,1,0:T(8,128)(2,1)}, bf16[4,256,1024]{2,1,0:T(8,128)(2,1)}) fusion(bf16[4,256,2048]{2,1,0:T(8,128)(2,1)} %param.16), kind=kLoop, calls=%fused_computation.94 | loop fusion | bytes 8388608 | tf_op jit(solution)/shard_map/slice | solution.py:38
  64.7 2.9 copy.109
  67.9 4.0 copy.110
  73.5 3.2 fusion.23
  76.7 82.3 %all-to-all-done = bf16[128,1,1,16,2048]{4,3,2,1,0:T(8,128)(2,1)} async-done(((bf16[128,1,1,16,2048]{4,3,2,1,0:T(8,128)(2,1)}), bf16[128,1,1,16,2048]{4,3,2,1,0:T(8,128)(2,1)}, u32[]{:S(2)}, u32[]{:S(2)}) %all-to-all-start) | async-done | bytes 8388640 | tf_op jit(solution)/shard_map/all_to_all | solution.py:102
  159.0 6.0 %fusion.52 = (bf16[1,4,512,1024]{3,2,1,0:T(8,128)(2,1)}, bf16[1,4,512,1024]{3,2,1,0:T(8,128)(2,1)}) fusion(bf16[1,4,512,2048]{3,2,1,0:T(8,128)(2,1)} %bitcast.10), kind=kLoop, calls=%fused_computation.93 | loop fusion | bytes 16777216 | tf_op jit(solution)/shard_map/gather | solution.py:104
  165.0 4.9 %gather_fusion.2 = bf16[4,512,1024]{2,1,0:T(8,128)(2,1)} fusion(bf16[1,4,512,1024]{3,2,1,0:T(8,128)(2,1)} %get-tuple-element.241, s32[4]{0:T(128)S(1)} %fusion.44), kind=kCustom, calls=%fused_computation.2 | custom fusion | bytes 8388640 | tf_op jit(solution)/shard_map/gather | solution.py:104
  170.0 5.0 %gather_fusion.3 = bf16[4,512,1024]{2,1,0:T(8,128)(2,1)} fusion(bf16[1,4,512,1024]{3,2,1,0:T(8,128)(2,1)} %get-tuple-element.242, s32[4]{0:T(128)S(1)} %fusion.44), kind=kCustom, calls=%fused_computation.3 | custom fusion | bytes 8388640 | tf_op jit(solution)/shard_map/gather | solution.py:104
  175.0 4.7 %maximum_select_fusion = bf16[4,512,2048]{2,1,0:T(8,128)(2,1)S(1)} fusion(bf16[4,512,1024]{2,1,0:T(8,128)(2,1)} %gather_fusion.3, bf16[4,512,1024]{2,1,0:T(8,128)(2,1)} %gather_fusion.2, pred[4,512]{1,0:T(4,128)(4,1)S(1)} %broadcast_compare_fusion), kind=kLoop, calls=%fused_computation.17 | loop fusion | flops 20971520 | bytes 16779264 | tf_op jit(solution)/shard_map/jit(_where)/select_n | solution.py:109
  179.7 4.1 fusion.51
  183.8 1.9 copy-done
  185.7 6.2 %copy.72 = bf16[4,512,1024]{1,2,0:T(8,128)(2,1)} copy(bf16[4,512,1024]{2,1,0:T(8,128)(2,1)} %get-tuple-element.240) | data formatting | bytes 8388608 | tf_op jit(solution)/shard_map/slice | solution.py:35
  191.9 6.3 %copy.80 = bf16[4,512,1024]{1,2,0:T(8,128)(2,1)} copy(bf16[4,512,1024]{2,1,0:T(8,128)(2,1)} %get-tuple-element.239) | data formatting | bytes 8388608 | tf_op jit(solution)/shard_map/slice | solution.py:38
  198.2 3.2 bitcast_reduce_fusion
  204.3 2.4 reshape.247
  207.1 4.3 fusion.56
  212.2 36.9 %all-gather.1 = f32[256,8,4,8]{3,1,2,0:T(8,128)S(1)} all-gather(f32[8,8,4,8]{3,1,2,0:T(8,128)S(1)} %copy.79), channel_id=3, replica_groups=mesh['src'=4,'seq'=32] {'seq'}, dimensions={0}, use_global_device_ids=true | all-gather | bytes 270336 | tf_op jit(solution)/shard_map/all_gather | solution.py:14
  249.2 34.4 %all-gather = f32[256,8,4,8]{3,1,2,0:T(8,128)S(1)} all-gather(f32[8,8,4,8]{3,1,2,0:T(8,128)S(1)} %copy.78), channel_id=2, replica_groups=mesh['src'=4,'seq'=32] {'seq'}, dimensions={0}, use_global_device_ids=true | all-gather | bytes 270336 | tf_op jit(solution)/shard_map/all_gather | solution.py:14
  283.6 2.0 copy-done.3
  285.7 52.9 %all-gather.5.cloned.1.call-done = f32[256,8,4,8,128]{4,3,2,1,0:T(8,128)} async-done(((f32[8,8,4,8,128]{4,3,2,1,0:T(8,128)}), f32[256,8,4,8,128]{4,3,2,1,0:T(8,128)}) %all-gather.5.cloned.1.call-update) | async-done | bytes 33554448 | tf_op jit(solution)/shard_map/all_gather | solution.py:14
  339.9 95.7 %while.19 = (s32[]{:T(128)}, f32[8,8,4,8]{3,2,1,0:T(4,128)S(1)}, f32[8,8,4,8]{3,2,1,0:T(4,128)S(1)}, f32[8,8,4,8,128]{4,3,2,1,0:T(8,128)S(1)}, f32[32,8,8,4,8]{4...) while((s32[]{:T(128)}, f32[8,8,4,8]{3,2,1,0:T(4,128)S(1)}, ...), condition=%wide.region_9.10_spmd, body=%wide.region_8.9_spmd.sunk | while | flops 798725 | bytes 3260567 | solution.py:19
  341.1 1.9 fusion.64
  344.2 1.9 fusion.64
  347.3 1.9 fusion.64
  350.4 1.9 fusion.64
  353.5 1.9 fusion.64
  356.6 1.9 fusion.64
  359.6 1.9 fusion.64
  362.7 1.9 fusion.64
  368.9 1.9 fusion.64
  372.0 1.9 fusion.64
  375.1 1.9 fusion.64
  390.5 1.9 fusion.64
  393.6 1.9 fusion.64
  396.7 1.9 fusion.64
  409.0 1.9 fusion.64
  412.1 1.9 fusion.64
  415.2 1.9 fusion.64
  427.5 1.9 fusion.64
  430.6 1.9 fusion.64
  433.7 1.9 fusion.64
  (147 shorter events, 73.0 us)
Async XLA Ops:
  46.4 12.2 %copy-start.8 = (s32[16]{0:T(128)S(1)}, s32[16]{0:T(128)}, u32[]{:S(2)}) copy-start(s32[16]{0:T(128)} %param.15) | copy-start | bytes 196
  46.4 12.4 %copy-start.4 = (bf16[8,4,8192]{2,1,0:T(4,128)(2,1)S(1)}, bf16[8,4,8192]{2,1,0:T(4,128)(2,1)}, u32[]{:S(2)}) copy-start(bf16[8,4,8192]{2,1,0:T(4,128)(2,1)} %param.18) | copy-start | bytes 1572868
  46.4 13.6 %copy-start.11 = (s32[16]{0:T(128)S(1)}, s32[16]{0:T(128)}, u32[]{:S(2)}) copy-start(s32[16]{0:T(128)} %param.17) | copy-start | bytes 196
  46.4 112.7 %all-to-all-start = ((bf16[128,1,1,16,2048]{4,3,2,1,0:T(8,128)(2,1)}), bf16[128,1,1,16,2048]{4,3,2,1,0:T(8,128)(2,1)}, u32[]{:S(2)}, u32[]{:S(2)}) async-start(bf16[128,1,1,16,2048]{4,3,2,1,0:T(8,128)(2,1)} %bitcast_select_fusion), calls=%async_computation | async-start | bytes 16777216 | tf_op jit(solution)/shard_map/all_to_all | solution.py:102
  58.3 280.2 %all-gather.5.cloned.1.call-start = ((), (), s32[]{:S(2)}) async-start(), calls=%async_computation.1 | async-start | bytes 34603008 | tf_op jit(solution)/shard_map/all_gather | solution.py:14
  64.7 7.9 %copy-start.9 = (s32[16]{0:T(128)S(1)}, s32[16]{0:T(128)}, u32[]{:S(2)}) copy-start(s32[16]{0:T(128)} %param.14) | copy-start | bytes 196
  179.7 6.0 %copy-start = (bf16[4,512,2048]{2,1,0:T(8,128)(2,1)}, bf16[4,512,2048]{2,1,0:T(8,128)(2,1)S(1)}, u32[]{:S(2)}) copy-start(bf16[4,512,2048]{2,1,0:T(8,128)(2,1)S(1)} %maximum_select_fusion) | copy-start | bytes 25165828
  191.9 6.3 %copy-start.7 = (bf16[4,4,8,8,128]{4,3,2,1,0:T(8,128)(2,1)S(1)}, bf16[4,4,8,8,128]{4,3,2,1,0:T(8,128)(2,1)}, u32[]{:S(2)}) copy-start(bf16[4,4,8,8,128]{4,3,2,1,0:T(8,128)(2,1)} %reshape.242) | copy-start | bytes 786436
  198.2 3.4 copy-start.1
  201.4 1.8 copy-start.5
  249.1 34.5 %copy-start.2 = (f32[256,8,4,8]{3,1,2,0:T(8,128)}, f32[256,8,4,8]{3,1,2,0:T(8,128)S(1)}, u32[]{:S(2)}) copy-start(f32[256,8,4,8]{3,1,2,0:T(8,128)S(1)} %all-gather.1) | copy-start | bytes 786436
  283.6 2.0 copy-start.3
  339.9 95.8 %copy-start.6 = (f32[8,8,4,8,4]{3,4,2,1,0:T(4,128)S(1)}, f32[8,8,4,8,4]{3,4,2,1,0:T(4,128)}, u32[]{:S(2)}) copy-start(f32[8,8,4,8,4]{3,4,2,1,0:T(4,128)} %get-tuple-element.254) | copy-start | bytes 98308
  339.9 96.3 %copy-start.10 = (bf16[8,4,2048]{2,1,0:T(4,128)(2,1)S(1)}, bf16[8,4,2048]{2,1,0:T(4,128)(2,1)}, u32[]{:S(2)}) copy-start(bf16[8,4,2048]{2,1,0:T(4,128)(2,1)} %param.19) | copy-start | bytes 393220
Sparse Core Ops, SparseCore 0:
  204.4 134.1 all-gather.4
where the time goes:
time: 448 us; the launch traced here: 445 us
  waiting for transfers between devices  135 us (30%)
  local copies, waits for them, and re-layouts  102 us (23%)
  other arithmetic  96 us (21%)
  blocking collectives  71.3 us (16%)
  between operations  14.3 us (3%)
  matrix products  13.9 us (3%)
  starting transfers between devices  12.2 us (3%)
    all_to_all x1, waiting for transfers between devices, on_device(): lax.all_to_all(flat_rows, ('src', 'seq'), split_axis=0, concat_axis=2, ti...  82.3 us
    all_gather x2, blocking collectives, combined_all(): gathered = jax.tree.map(lambda a: lax.all_gather(a, axis), part)  71.3 us
    add x31, other arithmetic, combine_states(): left_sum * left_factor[..., None] + right_sum * right_factor[..., None]  58.8 us
    all_gather x1, waiting for transfers between devices, combined_all(): gathered = jax.tree.map(lambda a: lax.all_gather(a, axis), part)  52.9 us
    dynamic_slice x34, local copies, waits for them, and re-layouts, take(): lax.dynamic_index_in_dim(a, source, 0, False)  32.1 us
    gather x3, local copies, waits for them, and re-layouts, on_device(): in_cache = pieces[from_pair, from_src]  15.9 us
    slice x3, local copies, waits for them, and re-layouts, partial_state(): cached_row_list[:, :, key_span_width:]  15.1 us
    gather x3, local copies, waits for them, and re-layouts, on_device(): jnp.take(restored_cache, send_order, axis=0)  13.8 us
  transfers between devices with their start and end apart: 2, of which 2 were waited for; matrix products, arithmetic and copies ran while one was open for 6% of the time, Pallas kernels for 0%

commit v1 on v0

v1 whole, which is shorter than its diff:
```python
import functools
import itertools
import math

import jax
import jax.numpy as jnp
from jax import lax
from jax.experimental import pallas as pl
from jax.experimental.pallas import tpu as pltpu
from jax.sharding import PartitionSpec as P

QUERY_HEADS = 64
KEY_VALUE_HEADS = 8
HEAD_SIZE = 128
GROUP = 16
N_SRC = 4
N_SEQ = 32
FEAT = 2048
KEY_WIDTH = KEY_VALUE_HEADS * HEAD_SIZE
MESH = pl.DeviceIdType.MESH
MIB = 2**20


def orbit(offset):
    y, x, z, core = offset
    found = []
    for sign in (1, -1):
        for turned in ((y, x, z), (z, y, x), (x, z, y)):
            found.append(tuple((sign * v) % 4 for v in turned) + (core,))
    return found


def send_offsets():
    every = [o for o in itertools.product(range(4), range(4), range(4), range(2)) if any(o)]
    hops = lambda o: sum(min(v, 4 - v) for v in o[:3])
    ordered = []
    for offset in sorted(every, key=lambda o: -hops(o)):
        for turned in orbit(offset):
            if turned not in ordered:
                ordered.append(turned)
    mixed = []
    for near in range(64):
        mixed.append(ordered[near])
        mixed.append(ordered[126 - near])
    return list(dict.fromkeys(mixed))


OFFSETS = send_offsets()


def own_place():
    src = lax.axis_index("src")
    seq = lax.axis_index("seq")
    return src, seq // 8, lax.rem(seq // 2, 4), lax.rem(seq, 2)


def place_at(own, offset):
    src, x, z, core = own
    dy, dx, dz, dcore = offset
    to_src = lax.rem(src + dy, 4) if dy else src
    to_x = lax.rem(x + dx, 4) if dx else x
    to_z = lax.rem(z + dz, 4) if dz else z
    to_core = 1 - core if dcore else core
    return to_src, to_x * 8 + to_z * 2 + to_core


WINDOW = 32


def move_kernel(
    assign, delta_hbm, anchors_hbm, scales_hbm, recv_hbm,
    delta, anchors, scales, anchor_rows, scale_rows, rebuilt,
    load_sem, own_sem, send_sem, recv_sem,
):
    own = own_place()
    src, seq = lax.axis_index("src"), lax.axis_index("seq")
    loads = [
        pltpu.make_async_copy(anchors_hbm, anchors, load_sem.at[0]),
        pltpu.make_async_copy(scales_hbm, scales, load_sem.at[1]),
        pltpu.make_async_copy(delta_hbm, delta, load_sem.at[2]),
    ]
    for load in loads:
        load.start()
    barrier = pltpu.get_barrier_semaphore()
    for offset in OFFSETS:
        pl.semaphore_signal(barrier, inc=1, device_id=place_at(own, offset), device_id_type=MESH)
    for load in loads:
        load.wait()
    for target in range(N_SRC):
        request = jnp.int32(0)
        for local in range(4):
            slot = assign[src * 4 + local]
            here = jnp.logical_and(slot >= target * 4, slot < target * 4 + 4)
            request = jnp.where(here, local, request)
        anchor_rows[...] = anchors[request].astype(jnp.float32)
        scale = scales[request]
        for head in range(FEAT // HEAD_SIZE):
            scale_rows[:, head * HEAD_SIZE : (head + 1) * HEAD_SIZE] = jnp.broadcast_to(
                scale[:, head : head + 1], (N_SEQ, HEAD_SIZE)
            )

        @pl.loop(0, N_SEQ)
        def _(group):
            rows = anchor_rows[pl.ds(group, 1), :] + scale_rows[pl.ds(group, 1), :] * delta[
                request, group
            ].astype(jnp.float32)
            rebuilt[target * N_SEQ + group] = rows.astype(jnp.bfloat16)

    mine = src * N_SEQ + seq
    keep = pltpu.make_async_copy(rebuilt.at[mine], recv_hbm.at[mine], own_sem)
    keep.start()
    pl.semaphore_wait(barrier, len(OFFSETS))
    copies = []
    for half in range(2):
        columns = pl.ds(half * (FEAT // 2), FEAT // 2)
        for offset in OFFSETS:
            to_src, to_seq = place_at(own, offset)
            number = len(copies)
            if number >= WINDOW:
                copies[number - WINDOW].wait_send()
            copy = pltpu.make_async_remote_copy(
                src_ref=rebuilt.at[to_src * N_SEQ + to_seq, :, columns],
                dst_ref=recv_hbm.at[mine, :, columns],
                send_sem=send_sem.at[number % WINDOW],
                recv_sem=recv_sem,
                device_id=(to_src, to_seq),
                device_id_type=MESH,
            )
            copy.start()
            copies.append(copy)
    for copy in copies[-WINDOW:]:
        copy.wait_send()
    arrived = recv_hbm.at[pl.ds(0, len(OFFSETS))]
    pltpu.make_async_copy(arrived, arrived, recv_sem).wait()
    keep.wait()


def move(assign, delta, anchors, scales):
    any_space = pl.BlockSpec(memory_space=pl.ANY)
    return pl.pallas_call(
        move_kernel,
        out_shape=jax.ShapeDtypeStruct((N_SRC * N_SEQ, GROUP, FEAT), jnp.bfloat16),
        in_specs=[pl.BlockSpec(memory_space=pltpu.SMEM)] + [any_space] * 3,
        out_specs=any_space,
        scratch_shapes=[
            pltpu.VMEM((4, N_SEQ, GROUP, FEAT), jnp.bfloat16),
            pltpu.VMEM((4, N_SEQ, FEAT), jnp.bfloat16),
            pltpu.VMEM((4, N_SEQ, FEAT // HEAD_SIZE), jnp.float32),
            pltpu.VMEM((N_SEQ, FEAT), jnp.float32),
            pltpu.VMEM((N_SEQ, FEAT), jnp.float32),
            pltpu.VMEM((N_SRC * N_SEQ, GROUP, FEAT), jnp.bfloat16),
            pltpu.SemaphoreType.DMA((3,)),
            pltpu.SemaphoreType.DMA,
            pltpu.SemaphoreType.DMA((WINDOW,)),
            pltpu.SemaphoreType.DMA,
        ],
        compiler_params=pltpu.CompilerParams(
            collective_id=1, has_side_effects=True, vmem_limit_bytes=48 * MIB
        ),
    )(assign, delta, anchors, scales)


SPAN = N_SEQ * GROUP
PLACE_ROWS = 256


def place_kernel(table, recv, out):
    slot, block = pl.program_id(0), pl.program_id(1)
    row = lax.broadcasted_iota(jnp.int32, (PLACE_ROWS, FEAT), 0)
    live = row < table[4 + slot] - block * PLACE_ROWS
    out[...] = jnp.where(live[None], recv[...], jnp.zeros_like(recv))


def place(table, recv):
    block = (1, PLACE_ROWS, FEAT)
    return pl.pallas_call(
        place_kernel,
        out_shape=jax.ShapeDtypeStruct((4, SPAN, FEAT), jnp.bfloat16),
        grid_spec=pltpu.PrefetchScalarGridSpec(
            num_scalar_prefetch=1,
            grid=(4, SPAN // PLACE_ROWS),
            in_specs=[pl.BlockSpec(block, lambda slot, part, table: (table[slot], part, 0))],
            out_specs=pl.BlockSpec(block, lambda slot, part, table: (slot, part, 0)),
        ),
        compiler_params=pltpu.CompilerParams(vmem_limit_bytes=32 * MIB),
    )(table, recv)


def partial_state(query_head_list, cached_row_list, valid_mask):
    slots = query_head_list.shape[0]
    keys = cached_row_list[:, :, :KEY_WIDTH].reshape(slots, -1, KEY_VALUE_HEADS, HEAD_SIZE)
    values = cached_row_list[:, :, KEY_WIDTH:].reshape(slots, -1, KEY_VALUE_HEADS, HEAD_SIZE)
    scores = jnp.einsum(
        "nhrd,nthd->nhrt", query_head_list, keys, preferred_element_type=jnp.float32
    ) / math.sqrt(HEAD_SIZE)
    keep_mask = valid_mask[:, None, None, :]
    scores = jnp.where(keep_mask, scores, -1e30)
    row_peak = jnp.max(scores, axis=-1)
    weights = jnp.where(keep_mask, jnp.exp(scores - row_peak[..., None]), 0.0)
    row_total = jnp.sum(weights, axis=-1)
    summed = jnp.einsum(
        "nhrt,nthd->nhrd", weights.astype(jnp.bfloat16), values, preferred_element_type=jnp.float32
    )
    return row_peak, row_total, summed


def on_device(
    kv_delta, anchors, scales, in_len, assign, res_cache, res_len, queries, fresh_key_value
):
    src = lax.axis_index("src")
    seq = lax.axis_index("seq")
    recv = move(
        assign,
        kv_delta.reshape(4, N_SEQ, GROUP, FEAT),
        anchors.reshape(4, N_SEQ, FEAT),
        scales.reshape(4, N_SEQ, FEAT // HEAD_SIZE),
    )
    slot_ids = src * 4 + jnp.arange(4)
    matches = assign[:, None] == slot_ids[None, :]
    slot_len = jnp.sum(jnp.where(matches, in_len[:, None], 0), axis=0)
    from_src = jnp.sum(jnp.where(matches, (jnp.arange(16) // 4)[:, None], 0), axis=0)
    table = jnp.concatenate([from_src, slot_len - seq * SPAN]).astype(jnp.int32)
    in_cache = place(table, recv.reshape(4, SPAN, FEAT))

    heads = queries.reshape(8, 4, KEY_VALUE_HEADS, 8, HEAD_SIZE).transpose(0, 2, 1, 3, 4)
    heads = heads.reshape(8, KEY_VALUE_HEADS, 32, HEAD_SIZE)
    res_own = lax.dynamic_slice_in_dim(res_len, src * 4, 4)
    in_valid = (seq * SPAN + jnp.arange(SPAN))[None, :] < slot_len[:, None]
    res_valid = (seq * 256 + jnp.arange(256))[None, :] < res_own[:, None]
    incoming = partial_state(heads[:4], in_cache, in_valid)
    resident = partial_state(heads[4:], res_cache, res_valid)
    peak, total, summed = [
        jnp.concatenate(pair, axis=0).reshape((N_SEQ, 64) + pair[0].shape[3:])
        for pair in zip(incoming, resident)
    ]
    stats = jnp.stack([peak, total], axis=1)
    stats, summed = [lax.all_to_all(a, "seq", 0, 0, tiled=True) for a in (stats, summed)]
    top = jnp.max(stats[:, 0], axis=0)
    factor = jnp.exp(stats[:, 0] - top)
    total = jnp.sum(stats[:, 1] * factor, axis=0)
    summed = jnp.sum(summed * factor[..., None], axis=0)
    row_peak, row_total, summed = [lax.all_gather(a, "seq") for a in (top, total, summed)]
    row_peak = row_peak.reshape(8, 8, 4, 8)
    row_total = row_total.reshape(8, 8, 4, 8)
    summed = summed.reshape(8, 8, 4, 8, HEAD_SIZE)

    query_head_list = queries.reshape(8, 4, KEY_VALUE_HEADS, 8, HEAD_SIZE)
    fresh_keys = fresh_key_value[:, :, :KEY_WIDTH].reshape(8, 4, KEY_VALUE_HEADS, HEAD_SIZE)
    fresh_values = fresh_key_value[:, :, KEY_WIDTH:].reshape(8, 4, KEY_VALUE_HEADS, HEAD_SIZE)
    new_scores = jnp.einsum(
        "nshgd,nthd->nhsgt", query_head_list, fresh_keys, preferred_element_type=jnp.float32
    ) / math.sqrt(HEAD_SIZE)
    causal = (jnp.arange(4)[None, :] <= jnp.arange(4)[:, None])[None, None, :, None, :]
    new_scores = jnp.where(causal, new_scores, -1e30)
    top_score = jnp.maximum(row_peak, jnp.max(new_scores, axis=-1))
    old_factor = jnp.exp(row_peak - top_score)
    new_weights = jnp.where(causal, jnp.exp(new_scores - top_score[..., None]), 0.0)
    row_total = row_total * old_factor + jnp.sum(new_weights, axis=-1)
    summed = summed * old_factor[..., None] + jnp.einsum(
        "nhsgt,nthd->nhsgd",
        new_weights.astype(jnp.bfloat16),
        fresh_values,
        preferred_element_type=jnp.float32,
    )
    result = (summed / row_total[..., None]).transpose(0, 2, 1, 3, 4).reshape(8, 4, -1)
    return in_cache, result.astype(jnp.bfloat16)


def solution(mesh):
    in_specs = (
        P("src", None, "seq", None, None),
        P("src", None, "seq", None),
        P("src", None, "seq", None),
        P(),
        P(),
        P("src", "seq", None),
        P(),
        P("src", None, None),
        P("src", None, None),
    )
    out_specs = (P("src", "seq", None), P("src", None, None))
    return jax.shard_map(
        on_device, mesh=mesh, in_specs=in_specs, out_specs=out_specs, check_vma=False
    )
```

time: 448 us -> 341 us (0.76)
  waiting for transfers between devices: 135 us -> 15.5 us
  Pallas kernels: 0 us -> 118 us
  other arithmetic: 96 us -> 5.64 us
  local copies, waits for them, and re-layouts: 102 us -> 30.2 us
  blocking collectives: 71.3 us -> 120 us
  starting transfers between devices: 12.2 us -> 17.5 us
    unnamed x0 -> x1, blocking collectives: none -> 120 us
    pallas_call x0 -> x2, Pallas kernels: none -> 118 us  [the longest x1 113 us: move(): pl.pallas_call(move_kernel, out_shape=jax.ShapeDtypeStruct((N_SRC * N_SEQ...]
    all_gather x2 -> x0, blocking collectives: 71.3 us -> none  [combined_all(): gathered = jax.tree.map(lambda a: lax.all_gather(a, axis), part)]
    all_to_all x1 -> x2, waiting for transfers between devices: 82.3 us -> 15.5 us  [on_device(): lax.all_to_all(a, 'seq', 0, 0, tiled=True)]
    add x66 -> x3, other arithmetic: 65.2 us -> 0.01 us  [the longest x1 0.01 us: on_device(): in_valid = (seq * SPAN + jnp.arange(SPAN))[None, :] < slot_len[:, None]]
    all_gather x1, waiting for transfers between devices: 52.9 us -> 0.02 us  [on_device(): lax.all_gather(a, 'seq')]
    dynamic_slice x36 -> x1, local copies, waits for them, and re-layouts: 32.9 us -> 0.07 us  [on_device(): res_own = lax.dynamic_slice_in_dim(res_len, src * 4, 4)]
    gather x6 -> x0, local copies, waits for them, and re-layouts: 29.7 us -> none  [the longest x3 15.9 us: on_device(): in_cache = pieces[from_pair, from_src]]
  transfers between devices with their start and end apart: 2 -> 3, of which waited for: 2 -> 1; matrix products, arithmetic and copies ran while one was open for 6% -> 4% of each run, Pallas kernels for 0% -> 0%
where the time goes in v1:
time: 341 us; the launch traced here: 336 us
  blocking collectives  120 us (35%)
  Pallas kernels  118 us (35%)
  local copies, waits for them, and re-layouts  30.2 us (9%)
  starting transfers between devices  17.5 us (5%)
  waiting for transfers between devices  15.5 us (5%)
  between operations  15 us (4%)
  matrix products  13.2 us (4%)
  other arithmetic  5.64 us (2%)
    unnamed x1, blocking collectives  120 us
    pallas_call x1, Pallas kernels, move(): pl.pallas_call(move_kernel, out_shape=jax.ShapeDtypeStruct((N_SRC * N_SEQ...  113 us
    unnamed x35, local copies, waits for them, and re-layouts  21.8 us
    all_to_all x2, starting transfers between devices, on_device(): lax.all_to_all(a, 'seq', 0, 0, tiled=True)  17.5 us
    all_to_all x2, waiting for transfers between devices, on_device(): lax.all_to_all(a, 'seq', 0, 0, tiled=True)  15.5 us
  transfers between devices with their start and end apart: 3, of which 1 were waited for; matrix products, arithmetic and copies ran while one was open for 4% of the time, Pallas kernels for 0%

profile of v1, /device:TPU:1, one launch (start us, length us, event | category | flops | bytes accessed | tf_op | source)
XLA Modules:
  0.0 335.5 jit_solution(2329010387570287824)
XLA Ops:
  7.2 0.9 fusion.40
  8.1 0.1 broadcast_compare_fusion
  8.2 0.8 copy.39
  9.0 1.6 reshape.196
  10.6 1.0 copy.77
  11.6 4.7 %fusion.47 = (bf16[4,256,1024]{2,1,0:T(8,128)(2,1)}, bf16[4,256,1024]{2,1,0:T(8,128)(2,1)}) fusion(bf16[4,256,2048]{2,1,0:T(8,128)(2,1)} %param.14), kind=kLoop, calls=%fused_computation.80 | loop fusion | bytes 8388608 | tf_op jit(solution)/shard_map/slice | solution.py:191
  16.3 2.9 copy.57
  19.3 0.1 pad_add_fusion.table
  19.3 112.9 %shard_map.104 = bf16[128,16,2048]{2,1,0:T(8,128)(2,1)} custom-call(s32[16]{0:T(128)S(1)} %copy-done.2, bf16[4,32,16,2048]{3,2,1,0:T(8,128)(2,1)} %bitcast.81, bf16[4,32,2048]{2,1,0:T(8,128)(2,1)S(1)} %bitcast.79, f32[4,32,16]{2,1,0:T(8,128)S(1)} %bitcast.80), custom_call_target="tpu_custom_call" | custom-call | tf_op jit(solution)/shard_map/pallas_call | solution.py:140
  132.2 3.4 %copy-done = bf16[128,16,2048]{2,1,0:T(8,128)(2,1)S(1)} copy-done((bf16[128,16,2048]{2,1,0:T(8,128)(2,1)S(1)}, bf16[128,16,2048]{2,1,0:T(8,128)(2,1)}, u32[]{:S(2)}) %copy-start) | copy-done | bytes 8388632
  135.6 5.1 %shard_map.105 = bf16[4,512,2048]{2,1,0:T(8,128)(2,1)} custom-call(s32[8]{0:T(128)S(1)} %pad_add_fusion.table, bf16[4,512,2048]{2,1,0:T(8,128)(2,1)S(1)} %bitcast.78), custom_call_target="tpu_custom_call" | custom-call | tf_op jit(solution)/shard_map/pallas_call | solution.py:176
  140.7 6.4 %slice_bitcast_fusion.1 = (bf16[4,64,8,8,128]{4,3,2,1,0:T(8,128)(2,1)}, bf16[4,64,8,8,128]{4,3,2,1,0:T(8,128)(2,1)}) fusion(bf16[4,512,2048]{2,1,0:T(8,128)(2,1)} %shard_map.105), kind=kLoop, calls=%fused_computation.7 | loop fusion | bytes 16777216
  147.2 0.1 dynamic_slice.3
  147.2 0.1 broadcast_compare_fusion.1
  147.3 1.6 fusion.49
  148.9 0.4 fusion.22
  149.3 0.2 copy-done.3
  149.6 2.6 bitcast_reduce_fusion
  152.2 1.3 copy-done.4
  153.5 0.7 fusion.8
  154.2 0.1 stack_reshape.6
  154.3 0.1 stack_reshape.7
  154.4 0.7 reshape.225
  155.1 9.9 %all-to-all-start.1 = ((f32[32,1,128]{2,1,0:T(1,128)}), f32[32,1,128]{2,1,0:T(1,128)S(1)}, u32[]{:S(2)}, u32[]{:S(2)}) async-start(f32[32,1,128]{2,1,0:T(1,128)} %reshape.225), calls=%async_computation.1 | async-start | bytes 32768 | tf_op jit(solution)/shard_map/all_to_all | solution.py:237
  165.1 2.9 copy.58
  167.9 0.8 fusion.24
  168.8 0.7 copy-done.5
  169.5 3.6 %fusion = f32[4,8,32,128]{3,2,1,0:T(8,128)S(1)} fusion(bf16[4,64,8,8,128]{4,3,2,1,0:T(8,128)(2,1)} %get-tuple-element.17, f32[4,8,512,32]{2,3,1,0:T(8,128)S(1)} %copy-done.5, f32[4,8,32]{2,1,0:T(8,128)S(1)} %get-tuple-element.24, pred[4,512]{1,0:T(4,128)(4,1)S(1)} %broadcast_compare_fusion), kind=kOutput, calls=%fused_computation | convolution fusion | flops 136839168 | bytes 6821888 | tf_op jit(solution)/shard_map/nhrt,nthd->nhrd/dot_general | solution.py:201
  173.1 1.1 pad_maximum_fusion
  174.2 7.5 %all-to-all-start = ((f32[32,64,128]{2,1,0:T(8,128)}), f32[32,64,128]{2,1,0:T(8,128)S(1)}, u32[]{:S(2)}, u32[]{:S(2)}) async-start(f32[32,64,128]{2,1,0:T(8,128)} %bitcast.10), calls=%async_computation | async-start | bytes 2097152 | tf_op jit(solution)/shard_map/all_to_all | solution.py:237
  181.7 0.0 all-gather.5.cloned.1.call-start
  181.8 0.5 broadcast.101
  182.3 0.7 reduce.1
  183.0 0.1 reshape.226
  183.2 15.5 %all-to-all-done = f32[32,64,128]{2,1,0:T(8,128)S(1)} async-done(((f32[32,64,128]{2,1,0:T(8,128)}), f32[32,64,128]{2,1,0:T(8,128)S(1)}, u32[]{:S(2)}, u32[]{:S(2)}) %all-to-all-start) | async-done | bytes 1048608 | tf_op jit(solution)/shard_map/all_to_all | solution.py:237
  198.7 1.0 multiply_reduce_fusion
  199.6 0.7 dynamic-slice
  201.0 2.5 fusion.50
  203.5 0.3 dynamic-update-slice
  203.8 0.3 dynamic-update-slice.1
  204.0 120.4 %all-reduce.2 = (f32[2048]{0:T(1024)S(1)}, f32[2048]{0:T(1024)S(1)}) all-reduce(f32[2048]{0:T(1024)S(1)} %dynamic-update-slice, f32[2048]{0:T(1024)S(1)} %dynamic-update-slice.1), channel_id=3, replica_groups=mesh['src'=4,'seq'=32] {'seq'}, use_global_device_ids=true, to_apply=%add | all-reduce | flops 4096 | bytes 32768
  324.4 0.2 reshape.202
  324.6 0.2 reshape.205
  324.8 0.5 fusion.30
  325.4 0.0 all-gather.5.cloned.1.call-done
  325.4 2.2 fusion.13
  327.6 0.1 copy.55
  327.8 0.9 reshape.224
  (36 shorter events, 0.3 us)
Async XLA Ops:
  10.6 5.7 %copy-start.6 = (bf16[8,4,8,8,128]{4,3,2,1,0:T(8,128)(2,1)}, bf16[8,4,8,8,128]{4,3,2,1,0:T(8,128)(2,1)S(1)}, u32[]{:S(2)}) copy-start(bf16[8,4,8,8,128]{4,3,2,1,0:T(8,128)(2,1)S(1)} %reshape.196) | copy-start | bytes 1572868
  16.3 3.0 copy-start.1
  16.3 3.0 copy-start.2
  132.2 3.4 %copy-start = (bf16[128,16,2048]{2,1,0:T(8,128)(2,1)S(1)}, bf16[128,16,2048]{2,1,0:T(8,128)(2,1)}, u32[]{:S(2)}) copy-start(bf16[128,16,2048]{2,1,0:T(8,128)(2,1)} %shard_map.104) | copy-start | bytes 25165828
  140.7 6.4 %copy-start.9 = (s32[16]{0:T(128)S(1)}, s32[16]{0:T(128)}, u32[]{:S(2)}) copy-start(s32[16]{0:T(128)} %param.15) | copy-start | bytes 196
  147.3 2.3 copy-start.3
  152.2 1.3 copy-start.4
  155.1 19.1 %all-to-all-start.1 = ((f32[32,1,128]{2,1,0:T(1,128)}), f32[32,1,128]{2,1,0:T(1,128)S(1)}, u32[]{:S(2)}, u32[]{:S(2)}) async-start(f32[32,1,128]{2,1,0:T(1,128)} %reshape.225), calls=%async_computation.1 | async-start | bytes 32768 | tf_op jit(solution)/shard_map/all_to_all | solution.py:237
  167.9 1.6 copy-start.5
  174.2 25.4 %copy-start.10 = (u32[128]{0:T(128)S(1)}, u32[128]{0:T(128)}, u32[]{:S(2)}) copy-start(u32[128]{0:T(128)} %constant.53) | copy-start | bytes 1540
  174.2 26.8 %copy-start.7 = (bf16[8,4,8,8,128]{4,3,2,1,0:T(8,128)(2,1)S(1)}, bf16[8,4,8,8,128]{4,3,2,1,0:T(8,128)(2,1)}, u32[]{:S(2)}) copy-start(bf16[8,4,8,8,128]{4,3,2,1,0:T(8,128)(2,1)} %copy-done.6) | copy-start | bytes 1572868
  174.2 26.8 %copy-start.8 = (bf16[8,4,2048]{2,1,0:T(4,128)(2,1)S(1)}, bf16[8,4,2048]{2,1,0:T(4,128)(2,1)}, u32[]{:S(2)}) copy-start(bf16[8,4,2048]{2,1,0:T(4,128)(2,1)} %param.17) | copy-start | bytes 393220
  174.2 24.4 %all-to-all-start = ((f32[32,64,128]{2,1,0:T(8,128)}), f32[32,64,128]{2,1,0:T(8,128)S(1)}, u32[]{:S(2)}, u32[]{:S(2)}) async-start(f32[32,64,128]{2,1,0:T(8,128)} %bitcast.10), calls=%async_computation | async-start | bytes 2097152 | tf_op jit(solution)/shard_map/all_to_all | solution.py:237
  181.7 143.7 %all-gather.5.cloned.1.call-start = ((), (), s32[]{:S(2)}) async-start(), calls=%async_computation.2 | async-start | bytes 1081344 | tf_op jit(solution)/shard_map/all_gather | solution.py:242
Sparse Core Ops, SparseCore 0:
  199.8 39.7 all-gather.4

commit v2 on v1

v2 whole, which is shorter than its diff:
```python
import functools
import itertools
import math

import jax
import jax.numpy as jnp
from jax import lax
from jax.experimental import pallas as pl
from jax.experimental.pallas import tpu as pltpu
from jax.sharding import PartitionSpec as P

QUERY_HEADS = 64
KEY_VALUE_HEADS = 8
HEAD_SIZE = 128
GROUP = 16
N_SRC = 4
N_SEQ = 32
FEAT = 2048
KEY_WIDTH = KEY_VALUE_HEADS * HEAD_SIZE
MESH = pl.DeviceIdType.MESH
MIB = 2**20


def orbit(offset):
    y, x, z, core = offset
    found = []
    for sign in (1, -1):
        for turned in ((y, x, z), (z, y, x), (x, z, y)):
            found.append(tuple((sign * v) % 4 for v in turned) + (core,))
    return found


def send_offsets():
    every = [o for o in itertools.product(range(4), range(4), range(4), range(2)) if any(o)]
    hops = lambda o: sum(min(v, 4 - v) for v in o[:3])
    ordered = []
    for offset in sorted(every, key=lambda o: -hops(o)):
        for turned in orbit(offset):
            if turned not in ordered:
                ordered.append(turned)
    mixed = []
    for near in range(64):
        mixed.append(ordered[near])
        mixed.append(ordered[126 - near])
    return list(dict.fromkeys(mixed))


OFFSETS = send_offsets()


def own_place():
    src = lax.axis_index("src")
    seq = lax.axis_index("seq")
    return src, seq // 8, lax.rem(seq // 2, 4), lax.rem(seq, 2)


def place_at(own, offset):
    src, x, z, core = own
    dy, dx, dz, dcore = offset
    to_src = lax.rem(src + dy, 4) if dy else src
    to_x = lax.rem(x + dx, 4) if dx else x
    to_z = lax.rem(z + dz, 4) if dz else z
    to_core = 1 - core if dcore else core
    return to_src, to_x * 8 + to_z * 2 + to_core

SPAN = N_SEQ * GROUP
RES_SPAN = 256
ROWS = 32
QUERY_ROWS = KEY_VALUE_HEADS * ROWS
CARD = QUERY_ROWS + KEY_VALUE_HEADS * GROUP
LOWEST = -1e30
WINDOW = 200
PUMP_BLOCK, PUMP_CORE, PUMP_PAIR, PUMP_RESULT = 4, 4, 8, 4
PLANE_OFFSETS = [o for o in OFFSETS if o[0] == 0 and o[3] == 0]
PLANE = 16


def remote(src_ref, dst_ref, send_sem, recv_sem, place):
    return pltpu.make_async_remote_copy(
        src_ref=src_ref,
        dst_ref=dst_ref,
        send_sem=send_sem,
        recv_sem=recv_sem,
        device_id=place,
        device_id_type=MESH,
    )


def take_bytes(ref, sem):
    pltpu.make_async_copy(ref, ref, sem).wait()


def partial_of(card, cache_keys, cache_values, live, first, head):
    query = card[pl.ds(pl.multiple_of(head * ROWS, ROWS), ROWS), :]
    fresh = card[pl.ds(pl.multiple_of(QUERY_ROWS + head * GROUP, GROUP), GROUP), :]
    across = (((1,), (1,)), ((), ()))
    unit = 1.0 / math.sqrt(HEAD_SIZE)
    scores = lax.dot_general(query, cache_keys, across, preferred_element_type=jnp.float32) * unit
    new_scores = lax.dot_general(query, fresh, across, preferred_element_type=jnp.float32) * unit
    step = lax.broadcasted_iota(jnp.int32, (ROWS, GROUP), 0) % 4
    token = lax.broadcasted_iota(jnp.int32, (ROWS, GROUP), 1)
    new_live = jnp.logical_and(token <= step, first)
    scores = jnp.where(live, scores, LOWEST)
    new_scores = jnp.where(new_live, new_scores, LOWEST)
    peak = jnp.maximum(
        jnp.max(scores, axis=1, keepdims=True), jnp.max(new_scores, axis=1, keepdims=True)
    )
    weights = jnp.where(live, jnp.exp(scores - peak), 0.0)
    new_weights = jnp.where(new_live, jnp.exp(new_scores - peak), 0.0)
    total = jnp.sum(weights, axis=1, keepdims=True) + jnp.sum(new_weights, axis=1, keepdims=True)
    summed = jnp.dot(
        weights.astype(jnp.bfloat16), cache_values, preferred_element_type=jnp.float32
    )
    rounded = new_weights.astype(jnp.bfloat16).astype(jnp.float32)
    fresh = fresh.astype(jnp.float32)
    for new in range(4):
        summed = summed + rounded[:, new : new + 1] * fresh[4 + new : 5 + new, :]
    return peak, total, summed


def read_cards(queries, fresh, cards):
    @pl.loop(0, 8)
    def _(slot):
        asked = queries[slot].astype(jnp.float32)
        new = fresh[slot].astype(jnp.float32)
        for head in range(KEY_VALUE_HEADS):
            rows = [
                asked[:, column * HEAD_SIZE : (column + 1) * HEAD_SIZE]
                for column in range(head * 8, head * 8 + 8)
            ]
            cards[slot, head * ROWS : (head + 1) * ROWS, :] = jnp.concatenate(
                rows, axis=0
            ).astype(jnp.bfloat16)
            low = head * HEAD_SIZE
            rows = [
                new[:, low : low + HEAD_SIZE],
                new[:, KEY_WIDTH + low : KEY_WIDTH + low + HEAD_SIZE],
                jnp.zeros((8, HEAD_SIZE), jnp.float32),
            ]
            begin = QUERY_ROWS + head * GROUP
            cards[slot, begin : begin + GROUP, :] = jnp.concatenate(rows, axis=0).astype(
                jnp.bfloat16
            )


def move_kernel(
    assign_hbm, in_len_hbm, res_len_hbm, delta_hbm, anchors_hbm, scales_hbm, resident_hbm, queries_hbm,
    fresh_hbm, recv_hbm, result_out,
    assign, in_len, res_len, delta, anchors, scales, resident, queries, fresh, cards, anchor_rows, scale_rows, rebuilt,
    cards_out, cards_in, part_out, stat_out, core_part, core_stat, joint_part, joint_stat,
    part_in, stat_in, factors, result, unused,
    load_sem, own_sem, send_sem, recv_sem, card_send, card_recv, core_send, core_recv,
    pair_send, pair_recv, result_send, result_recv, back_send, back_recv,
):
    own = own_place()
    src, seq = lax.axis_index("src"), lax.axis_index("seq")
    x, z, core = own[1:]
    plane = x * 4 + z
    sibling = (src, seq + 1 - 2 * core)
    loads = [
        pltpu.make_async_copy(anchors_hbm, anchors, load_sem.at[0]),
        pltpu.make_async_copy(scales_hbm, scales, load_sem.at[1]),
        pltpu.make_async_copy(delta_hbm, delta, load_sem.at[2]),
        pltpu.make_async_copy(queries_hbm, queries, load_sem.at[3]),
        pltpu.make_async_copy(fresh_hbm, fresh, load_sem.at[4]),
        pltpu.make_async_copy(resident_hbm, resident, load_sem.at[5]),
        pltpu.make_async_copy(assign_hbm, assign, load_sem.at[6]),
        pltpu.make_async_copy(in_len_hbm, in_len, load_sem.at[7]),
        pltpu.make_async_copy(res_len_hbm, res_len, load_sem.at[8]),
    ]
    for load in loads:
        load.start()
    barrier = pltpu.get_barrier_semaphore()
    for offset in OFFSETS:
        pl.semaphore_signal(barrier, inc=1, device_id=place_at(own, offset), device_id_type=MESH)
    for load in loads[:3] + loads[6:]:
        load.wait()
    same_group = lax.broadcasted_iota(jnp.int32, (N_SEQ, N_SEQ), 0) == lax.broadcasted_iota(
        jnp.int32, (N_SEQ, N_SEQ), 1
    )
    lengths = []
    for target in range(N_SRC):
        request, length = jnp.int32(0), jnp.int32(0)
        for local in range(4):
            slot = assign[src * 4 + local]
            here = jnp.logical_and(slot >= target * 4, slot < target * 4 + 4)
            request = jnp.where(here, local, request)
            length = jnp.where(here, in_len[src * 4 + local], length)
        lengths.append(length)
        anchor_rows[...] = anchors[request].astype(jnp.float32)
        scale = scales[request]
        for head in range(FEAT // HEAD_SIZE):
            column = jnp.sum(
                jnp.where(same_group, scale[head : head + 1, :], 0.0), axis=1, keepdims=True
            )
            scale_rows[:, head * HEAD_SIZE : (head + 1) * HEAD_SIZE] = jnp.broadcast_to(
                column, (N_SEQ, HEAD_SIZE)
            )

        @pl.loop(0, N_SEQ)
        def _(group):
            rows = anchor_rows[pl.ds(group, 1), :] + scale_rows[pl.ds(group, 1), :] * delta[
                request, group
            ].reshape(GROUP, FEAT).astype(jnp.float32)
            rebuilt[target, pl.ds(pl.multiple_of(group * GROUP, GROUP), GROUP), :] = rows.astype(
                jnp.bfloat16
            )

    for load in loads[3:5]:
        load.wait()
    read_cards(queries, fresh, cards)
    for source in range(N_SRC):
        place = jnp.int32(0)
        for local in range(4):
            slot = assign[source * 4 + local] - src * 4
            place = jnp.where(jnp.logical_and(slot >= 0, slot < 4), slot, place)
        cards_out[source] = cards[place]
    cards_in[src] = cards_out[src]

    mine = src * N_SEQ + seq
    keep = pltpu.make_async_copy(
        rebuilt.at[src, pl.ds(pl.multiple_of(seq * GROUP, GROUP), GROUP), :],
        recv_hbm.at[mine],
        own_sem,
    )
    keep.start()
    pl.semaphore_wait(barrier, len(OFFSETS))

    card_copies = []
    for turn in range(1, N_SRC):
        to_src = lax.rem(src + turn, N_SRC)
        card_copies.append(
            remote(
                cards_out.at[to_src], cards_in.at[src],
                card_send.at[turn - 1], card_recv.at[turn - 1], (to_src, seq),
            )
        )
        card_copies[-1].start()

    copies = []
    work = [(half, offset) for half in range(2) for offset in OFFSETS]

    def pump(count):
        for half, offset in work[len(copies) : len(copies) + count]:
            to_src, to_seq = place_at(own, offset)
            columns = pl.ds(half * (FEAT // 2), FEAT // 2)
            number = len(copies)
            if number >= WINDOW:
                copies[number - WINDOW].wait_send()
            copy = remote(
                rebuilt.at[to_src, pl.ds(pl.multiple_of(to_seq * GROUP, GROUP), GROUP), columns],
                recv_hbm.at[mine, :, columns],
                send_sem.at[number % WINDOW],
                recv_sem,
                (to_src, to_seq),
            )
            copy.start()
            copies.append(copy)

    pump(WINDOW)
    for copy in card_copies:
        copy.wait()
    loads[5].wait()

    first = seq == 0
    ahead = lax.broadcasted_iota(jnp.int32, (1, SPAN), 1)
    in_position = ahead // GROUP * SPAN + seq * GROUP + ahead % GROUP
    res_position = seq * RES_SPAN + lax.broadcasted_iota(jnp.int32, (1, RES_SPAN), 1)
    row_id = lax.broadcasted_iota(jnp.int32, (ROWS, HEAD_SIZE), 0)
    lane_id = lax.broadcasted_iota(jnp.int32, (ROWS, HEAD_SIZE), 1)
    for block in range(4):
        in_live = in_position < lengths[block]
        res_live = res_position < res_len[src * 4 + block]
        for start in (0, 4):

            @pl.loop(start, start + 4)
            def _(head):
                keys = pl.ds(pl.multiple_of(head * HEAD_SIZE, HEAD_SIZE), HEAD_SIZE)
                values = pl.ds(pl.multiple_of(KEY_WIDTH + head * HEAD_SIZE, HEAD_SIZE), HEAD_SIZE)
                in_peak, in_total, in_sum = partial_of(
                    cards_in.at[block], rebuilt[block, :, keys], rebuilt[block, :, values],
                    in_live, first, head,
                )
                res_peak, res_total, res_sum = partial_of(
                    cards.at[4 + block], resident[block, :, keys], resident[block, :, values],
                    res_live, first, head,
                )
                to_core, to_plane = head % 2, block * 4 + head // 2
                part_out[to_core, to_plane, 0] = in_sum.astype(jnp.bfloat16)
                part_out[to_core, to_plane, 1] = res_sum.astype(jnp.bfloat16)
                held = jnp.where(
                    lane_id < 64,
                    jnp.where(lane_id < 32, in_peak, in_total),
                    jnp.where(lane_id < 96, res_peak, res_total),
                )
                stat_out[to_core, to_plane] = jnp.sum(
                    jnp.where(lane_id % ROWS == row_id, held, 0.0), axis=0, keepdims=True
                )

            pump(PUMP_BLOCK)

    core_copies = [
        remote(
            stat_out.at[1 - core], core_stat, core_send.at[0], core_recv.at[0], sibling
        ),
        remote(
            part_out.at[1 - core], core_part, core_send.at[1], core_recv.at[1], sibling
        ),
    ]
    for copy in core_copies:
        copy.start()
    pump(PUMP_CORE)
    for copy in core_copies:
        copy.wait()

    def columns_of(row):
        return [
            jnp.sum(jnp.where(lane_id == row_id + lane, row, 0.0), axis=1, keepdims=True)
            for lane in (0, 64)
        ]

    stat_lane = lax.broadcasted_iota(jnp.int32, (1, HEAD_SIZE), 1)
    is_peak = stat_lane % 64 < 32

    @pl.loop(0, PLANE)
    def _(pair):
        here, there = stat_out[core, pair], core_stat[pair]
        peak = jnp.maximum(here, there)
        here_factor, there_factor = jnp.exp(here - peak), jnp.exp(there - peak)
        total = here * pltpu.roll(here_factor, ROWS, 1) + there * pltpu.roll(there_factor, ROWS, 1)
        joint_stat[pair] = jnp.where(is_peak, peak, total)
        here_columns, there_columns = columns_of(here_factor), columns_of(there_factor)
        for kind in range(2):
            joint_part[pair, kind] = (
                here_columns[kind] * part_out[core, pair, kind].astype(jnp.float32)
                + there_columns[kind] * core_part[pair, kind].astype(jnp.float32)
            ).astype(jnp.bfloat16)

    part_in[plane] = joint_part[plane]
    stat_in[plane] = joint_stat[plane]
    for offset in PLANE_OFFSETS:
        place = place_at(own, offset)
        to_plane = place[1] // 2
        remote(
            joint_stat.at[to_plane], stat_in.at[plane], pair_send.at[0], pair_recv.at[0], place
        ).start()
        remote(
            joint_part.at[to_plane], part_in.at[plane], pair_send.at[1], pair_recv.at[1], place
        ).start()
    pump(PUMP_PAIR)
    others = pl.ds(0, PLANE - 1)
    take_bytes(stat_in.at[others], pair_recv.at[0])
    take_bytes(part_in.at[others], pair_recv.at[1])
    stats = jnp.concatenate([stat_in[device] for device in range(PLANE)], axis=0)
    factor = jnp.exp(stats - jnp.max(stats, axis=0, keepdims=True))
    totals = pltpu.roll(stats, HEAD_SIZE - ROWS, 1)
    factors[...] = factor / jnp.sum(factor * totals, axis=0, keepdims=True)

    def add(device, sums):
        columns = columns_of(factors[pl.ds(device, 1), :])
        return tuple(
            sums[kind] + columns[kind] * part_in[device, kind].astype(jnp.float32)
            for kind in range(2)
        )

    zero = jnp.zeros((ROWS, HEAD_SIZE), jnp.float32)
    sums = lax.fori_loop(0, PLANE, add, (zero, zero))
    for kind in range(2):
        result[kind] = sums[kind].astype(jnp.bfloat16)

    row = src * 4 + z
    at_home = pltpu.make_async_copy(result.at[1], result_out.at[1, core, plane], own_sem)

    @pl.when(x == src)
    def _():
        pltpu.make_async_copy(result.at[0], result_out.at[0, core, row], result_recv.at[0]).start()
        pltpu.make_async_copy(result.at[0], unused, result_send.at[0]).start()

    @pl.when(x != src)
    def _():
        remote(
            result.at[0], result_out.at[0, core, row], result_send.at[0], result_recv.at[0],
            (x, seq),
        ).start()

    for offset in PLANE_OFFSETS:
        to_seq = place_at(own, offset)[1]
        remote(
            result.at[0], result_out.at[0, core, row], result_send.at[0], result_recv.at[0],
            (x, to_seq),
        ).start()
        remote(
            result.at[1], result_out.at[1, core, plane], result_send.at[1], result_recv.at[1],
            (src, to_seq),
        ).start()
    keep.wait()
    at_home.start()
    pump(PUMP_RESULT)
    at_home.wait()
    take_bytes(result_out.at[0, core], result_recv.at[0])
    take_bytes(result_out.at[1, core, others], result_recv.at[1])
    back_copies = [
        remote(
            result_out.at[kind, core], result_out.at[kind, core],
            back_send.at[kind], back_recv.at[kind], sibling,
        )
        for kind in range(2)
    ]
    for copy in back_copies:
        copy.start()
    pump(len(work))
    take_bytes(stat_in.at[others], pair_send.at[0])
    take_bytes(part_in.at[others], pair_send.at[1])
    take_bytes(result_out.at[0, core], result_send.at[0])
    take_bytes(result_out.at[1, core, others], result_send.at[1])
    for copy in back_copies:
        copy.wait()
    for copy in copies[-WINDOW:]:
        copy.wait_send()
    take_bytes(recv_hbm.at[pl.ds(0, len(OFFSETS))], recv_sem)


def move(assign, in_len, res_len, delta, anchors, scales, resident, queries, fresh):
    any_space = pl.BlockSpec(memory_space=pl.ANY)
    bf16, f32 = jnp.bfloat16, jnp.float32
    operands = [
        pltpu.with_memory_space_constraint(a, pltpu.HBM)
        for a in (assign, in_len, res_len, delta, anchors, scales, resident, queries, fresh)
    ]
    return pl.pallas_call(
        move_kernel,
        out_shape=(
            pltpu.VMEM((N_SRC * N_SEQ, GROUP, FEAT), bf16),
            pltpu.VMEM((2, 2, PLANE, ROWS, HEAD_SIZE), bf16),
        ),
        in_specs=[pl.BlockSpec(memory_space=pltpu.HBM)] * 9,
        out_specs=(any_space, any_space),
        scratch_shapes=[
            pltpu.SMEM((16,), jnp.int32),
            pltpu.SMEM((16,), jnp.int32),
            pltpu.SMEM((16,), jnp.int32),
            pltpu.VMEM(delta.shape, bf16),
            pltpu.VMEM(anchors.shape, bf16),
            pltpu.VMEM(scales.shape, f32),
            pltpu.VMEM(resident.shape, bf16),
            pltpu.VMEM(queries.shape, bf16),
            pltpu.VMEM(fresh.shape, bf16),
            pltpu.VMEM((8, CARD, HEAD_SIZE), bf16),
            pltpu.VMEM((N_SEQ, FEAT), f32),
            pltpu.VMEM((N_SEQ, FEAT), f32),
            pltpu.VMEM((N_SRC, SPAN, FEAT), bf16),
            pltpu.VMEM((N_SRC, CARD, HEAD_SIZE), bf16),
            pltpu.VMEM((N_SRC, CARD, HEAD_SIZE), bf16),
            pltpu.VMEM((2, PLANE, 2, ROWS, HEAD_SIZE), bf16),
            pltpu.VMEM((2, PLANE, 1, HEAD_SIZE), f32),
            pltpu.VMEM((PLANE, 2, ROWS, HEAD_SIZE), bf16),
            pltpu.VMEM((PLANE, 1, HEAD_SIZE), f32),
            pltpu.VMEM((PLANE, 2, ROWS, HEAD_SIZE), bf16),
            pltpu.VMEM((PLANE, 1, HEAD_SIZE), f32),
            pltpu.VMEM((PLANE, 2, ROWS, HEAD_SIZE), bf16),
            pltpu.VMEM((PLANE, 1, HEAD_SIZE), f32),
            pltpu.VMEM((PLANE, HEAD_SIZE), f32),
            pltpu.VMEM((2, ROWS, HEAD_SIZE), bf16),
            pltpu.VMEM((ROWS, HEAD_SIZE), bf16),
            pltpu.SemaphoreType.DMA((9,)),
            pltpu.SemaphoreType.DMA,
            pltpu.SemaphoreType.DMA((WINDOW,)),
            pltpu.SemaphoreType.DMA,
            pltpu.SemaphoreType.DMA((3,)),
            pltpu.SemaphoreType.DMA((3,)),
            pltpu.SemaphoreType.DMA((2,)),
            pltpu.SemaphoreType.DMA((2,)),
            pltpu.SemaphoreType.DMA((2,)),
            pltpu.SemaphoreType.DMA((2,)),
            pltpu.SemaphoreType.DMA((2,)),
            pltpu.SemaphoreType.DMA((2,)),
            pltpu.SemaphoreType.DMA((2,)),
            pltpu.SemaphoreType.DMA((2,)),
        ],
        compiler_params=pltpu.CompilerParams(
            collective_id=1, has_side_effects=True, vmem_limit_bytes=32 * MIB
        ),
    )(*operands)


EDGE = 64


def place_kernel(
    assign_hbm, in_len_hbm, recv, result, in_cache, attention,
    assign, in_len, zeros, edge, out_sem, edge_sem, load_sem,
):
    src, seq = lax.axis_index("src"), lax.axis_index("seq")
    loads = [
        pltpu.make_async_copy(assign_hbm, assign, load_sem.at[0]),
        pltpu.make_async_copy(in_len_hbm, in_len, load_sem.at[1]),
    ]
    for load in loads:
        load.start()
    for load in loads:
        load.wait()
    zeros[...] = jnp.zeros_like(zeros)
    sources, counts = [], []
    for slot in range(4):
        source, length = jnp.int32(0), jnp.int32(0)
        for request in range(16):
            here = assign[request] == src * 4 + slot
            source = jnp.where(here, request // 4, source)
            length = jnp.where(here, in_len[request], length)
        count = jnp.clip(length - seq * SPAN, 0, SPAN)
        sources.append(source)
        counts.append(count)
        whole = count // EDGE
        cut = whole * EDGE < count
        for part in range(SPAN // EDGE):
            rows = pl.ds(part * EDGE, EDGE)

            @pl.when(part < whole)
            def _():
                pltpu.make_async_copy(
                    recv.at[source, rows], in_cache.at[slot, rows], out_sem
                ).start()

            @pl.when(jnp.logical_and(part == whole, cut))
            def _():
                pltpu.make_async_copy(recv.at[source, rows], edge.at[slot], edge_sem.at[slot]).start()

            @pl.when(jnp.logical_and(part >= whole, jnp.logical_or(part > whole, ~cut)))
            def _():
                pltpu.make_async_copy(zeros, in_cache.at[slot, rows], out_sem).start()

    row = lax.broadcasted_iota(jnp.int32, (EDGE, FEAT), 0)
    for slot in range(4):
        whole = counts[slot] // EDGE

        @pl.when(whole * EDGE < counts[slot])
        def _():
            pltpu.make_async_copy(edge.at[slot], edge.at[slot], edge_sem.at[slot]).wait()
            kept = edge[slot]
            edge[slot] = jnp.where(row < counts[slot] - whole * EDGE, kept, jnp.zeros_like(kept))
            rows = pl.ds(pl.multiple_of(whole * EDGE, EDGE), EDGE)
            pltpu.make_async_copy(edge.at[slot], in_cache.at[slot, rows], out_sem).start()

    for slot in range(8):
        for head in range(KEY_VALUE_HEADS):
            first = sources[slot] if slot < 4 else slot - 4
            rows = result[slot // 4, head % 2, first * 4 + head // 2].astype(jnp.float32)
            for column in range(8):
                low = (head * 8 + column) * HEAD_SIZE
                attention[slot, :, low : low + HEAD_SIZE] = rows[
                    column * 4 : column * 4 + 4, :
                ].astype(jnp.bfloat16)
    pltpu.make_async_copy(in_cache, in_cache, out_sem).wait()


def place(assign, in_len, recv, result):
    scalars = pl.BlockSpec(memory_space=pltpu.HBM)
    whole = pl.BlockSpec(memory_space=pltpu.VMEM)
    any_space = pl.BlockSpec(memory_space=pl.ANY)
    return pl.pallas_call(
        place_kernel,
        out_shape=(
            jax.ShapeDtypeStruct((4, SPAN, FEAT), jnp.bfloat16),
            jax.ShapeDtypeStruct((8, 4, QUERY_HEADS * HEAD_SIZE), jnp.bfloat16),
        ),
        in_specs=[scalars, scalars, any_space, whole],
        out_specs=(any_space, whole),
        scratch_shapes=[
            pltpu.SMEM((16,), jnp.int32),
            pltpu.SMEM((16,), jnp.int32),
            pltpu.VMEM((EDGE, FEAT), jnp.bfloat16),
            pltpu.VMEM((4, EDGE, FEAT), jnp.bfloat16),
            pltpu.SemaphoreType.DMA,
            pltpu.SemaphoreType.DMA((4,)),
            pltpu.SemaphoreType.DMA((2,)),
        ],
        compiler_params=pltpu.CompilerParams(vmem_limit_bytes=16 * MIB),
    )(
        pltpu.with_memory_space_constraint(assign, pltpu.HBM),
        pltpu.with_memory_space_constraint(in_len, pltpu.HBM),
        recv,
        result,
    )


def on_device(
    kv_delta, anchors, scales, in_len, assign, res_cache, res_len, queries, fresh_key_value
):
    recv, result = move(
        assign,
        in_len,
        res_len,
        kv_delta.reshape(4, N_SEQ, GROUP, FEAT),
        anchors.reshape(4, N_SEQ, FEAT),
        scales.reshape(4, N_SEQ, FEAT // HEAD_SIZE).transpose(0, 2, 1),
        res_cache,
        queries,
        fresh_key_value,
    )
    return place(assign, in_len, recv.reshape(4, SPAN, FEAT), result)


def solution(mesh):
    in_specs = (
        P("src", None, "seq", None, None),
        P("src", None, "seq", None),
        P("src", None, "seq", None),
        P(),
        P(),
        P("src", "seq", None),
        P(),
        P("src", None, None),
        P("src", None, None),
    )
    out_specs = (P("src", "seq", None), P("src", None, None))
    return jax.shard_map(
        on_device, mesh=mesh, in_specs=in_specs, out_specs=out_specs, check_vma=False
    )
```

time: 341 us -> 127 us (0.37); the launches traced: 336 us -> 127 us
  blocking collectives: 120 us -> 0 us
  local copies, waits for them, and re-layouts: 30.2 us -> 0 us
  starting transfers between devices: 17.5 us -> 0 us
  waiting for transfers between devices: 15.5 us -> 0 us
  between operations: 15 us -> 0.64 us
  matrix products: 13.2 us -> 0 us
  Pallas kernels: 118 us -> 126 us
  other arithmetic: 5.64 us -> 0 us
    unnamed x1 -> x0, blocking collectives: 120 us -> none
    unnamed x35 -> x0, local copies, waits for them, and re-layouts: 21.8 us -> none
    all_to_all x2 -> x0, starting transfers between devices: 17.5 us -> none  [on_device(): lax.all_to_all(a, 'seq', 0, 0, tiled=True)]
    all_to_all x2 -> x0, waiting for transfers between devices: 15.5 us -> none  [on_device(): lax.all_to_all(a, 'seq', 0, 0, tiled=True)]
    dot_general x6 -> x0, matrix products: 13.2 us -> none  [the longest x2 4.43 us: partial_state(): jnp.einsum('nhrt,nthd->nhrd', weights.astype(jnp.bfloat16), values, prefe...]
    pallas_call x2, Pallas kernels: 118 us -> 126 us  [the longest x1 121 us: move(): pl.pallas_call(move_kernel, out_shape=(pltpu.VMEM((N_SRC * N_SEQ, GROUP,...]
    slice x2 -> x0, local copies, waits for them, and re-layouts: 4.77 us -> none  [the longest x1 4.74 us: partial_state(): cached_row_list[:, :, :KEY_WIDTH]]
    reduce_sum x6 -> x0, other arithmetic: 3.46 us -> none  [the longest x2 1.07 us: partial_state(): row_total = jnp.sum(weights, axis=-1)]
  transfers between devices with their start and end apart: 3 -> 0, of which waited for: 1 -> 0; matrix products, arithmetic and copies ran while one was open for 4% -> 0% of each run, Pallas kernels for 0% -> 0%
where the time goes in v2:
time: 127 us
  Pallas kernels  126 us (99%)
    pallas_call x1, Pallas kernels, move(): pl.pallas_call(move_kernel, out_shape=(pltpu.VMEM((N_SRC * N_SEQ, GROUP,...  121 us
    pallas_call x1, Pallas kernels, place(): pl.pallas_call(place_kernel, out_shape=(jax.ShapeDtypeStruct((4, SPAN, FE...  4.81 us

profile of v2, /device:TPU:1, one launch (start us, length us, event | category | flops | bytes accessed | tf_op | source)
XLA Modules:
  0.0 126.7 jit_solution(9329034293760553116)
XLA Ops:
  0.6 121.3 %shard_map.104 = (bf16[128,16,2048]{2,1,0:T(8,128)(2,1)S(1)}, bf16[2,2,16,32,128]{4,3,2,1,0:T(8,128)(2,1)S(1)}) custom-call(s32[16]{0:T(128)} %assign_hbm.3, s32[16]{0:T(128)} %in_len_hbm.3, s32[16]{0:T(128)} %res_len_hbm.1, bf16[4,32,16,2048]{3,2,1,0:T(8,128)(2,1)} %bitcast.7, bf16[4,32,2048]{2,1,0:T(8,128)(2,1)} %bitcast.8, f32[4,16,32]{2,1,0:T(8,128)} %bitcast.9, ...), custom_call_target="tpu_custom_call" | custom-call | tf_op jit(solution)/shard_map/pallas_call | solution.py:430
  121.9 4.8 %shard_map.105 = (bf16[4,512,2048]{2,1,0:T(8,128)(2,1)}, bf16[8,4,8192]{2,1,0:T(4,128)(2,1)}) custom-call(s32[16]{0:T(128)} %assign_hbm.3, s32[16]{0:T(128)} %in_len_hbm.3, bf16[4,512,2048]{2,1,0:T(8,128)(2,1)S(1)} %bitcast.6, bf16[2,2,16,32,128]{4,3,2,1,0:T(8,128)(2,1)S(1)} %get-tuple-element.5.result), custom_call_target="tpu_custom_call" | custom-call | tf_op jit(solution)/shard_map/pallas_call | solution.py:560

commit v3 on v2

--- a/solution.py
+++ b/solution.py
@@ -67,10 +67,10 @@
 RES_SPAN = 256
 ROWS = 32
 QUERY_ROWS = KEY_VALUE_HEADS * ROWS
-CARD = QUERY_ROWS + KEY_VALUE_HEADS * GROUP
+NEW_ROWS = KEY_VALUE_HEADS * GROUP
 LOWEST = -1e30
-WINDOW = 200
-PUMP_BLOCK, PUMP_CORE, PUMP_PAIR, PUMP_RESULT = 4, 4, 8, 4
+WINDOW = 170
+PUMP_FIRST, PUMP_BLOCK, PUMP_CORE, PUMP_PAIR = 40, 8, 6, 8
 PLANE_OFFSETS = [o for o in OFFSETS if o[0] == 0 and o[3] == 0]
 PLANE = 16
 
@@ -90,9 +90,10 @@
     pltpu.make_async_copy(ref, ref, sem).wait()
 
 
-def partial_of(card, cache_keys, cache_values, live, first, head):
+def partial_of(card, news, cache_keys, cache_values, live, first, head):
     query = card[pl.ds(pl.multiple_of(head * ROWS, ROWS), ROWS), :]
-    fresh = card[pl.ds(pl.multiple_of(QUERY_ROWS + head * GROUP, GROUP), GROUP), :]
+    fresh = news[pl.ds(pl.multiple_of(head * GROUP, GROUP), GROUP), :]
+    fresh = jnp.where(first, fresh, jnp.zeros_like(fresh))
     across = (((1,), (1,)), ((), ()))
     unit = 1.0 / math.sqrt(HEAD_SIZE)
     scores = lax.dot_general(query, cache_keys, across, preferred_element_type=jnp.float32) * unit
@@ -118,7 +119,7 @@
     return peak, total, summed
 
 
-def read_cards(queries, fresh, cards):
+def read_cards(queries, fresh, cards, news):
     @pl.loop(0, 8)
     def _(slot):
         asked = queries[slot].astype(jnp.float32)
@@ -137,19 +138,18 @@
                 new[:, KEY_WIDTH + low : KEY_WIDTH + low + HEAD_SIZE],
                 jnp.zeros((8, HEAD_SIZE), jnp.float32),
             ]
-            begin = QUERY_ROWS + head * GROUP
-            cards[slot, begin : begin + GROUP, :] = jnp.concatenate(rows, axis=0).astype(
-                jnp.bfloat16
-            )
+            news[slot, head * GROUP : (head + 1) * GROUP, :] = jnp.concatenate(
+                rows, axis=0
+            ).astype(jnp.bfloat16)
 
 
 def move_kernel(
     assign_hbm, in_len_hbm, res_len_hbm, delta_hbm, anchors_hbm, scales_hbm, resident_hbm, queries_hbm,
     fresh_hbm, recv_hbm, result_out,
-    assign, in_len, res_len, delta, anchors, scales, resident, queries, fresh, cards, anchor_rows, scale_rows, rebuilt,
-    cards_out, cards_in, part_out, stat_out, core_part, core_stat, joint_part, joint_stat,
+    assign, in_len, res_len, delta, anchors, scales, resident, queries, fresh, cards, news, anchor_rows, scale_rows, rebuilt,
+    cards_out, cards_in, news_out, news_in, part_out, stat_out, core_part, core_stat, joint_part, joint_stat,
     part_in, stat_in, factors, result, unused,
-    load_sem, own_sem, send_sem, recv_sem, card_send, card_recv, core_send, core_recv,
+    load_sem, own_sem, send_sem, recv_sem, card_send, card_recv, new_send, new_recv, swap_send, swap_recv, core_send, core_recv,
     pair_send, pair_recv, result_send, result_recv, back_send, back_recv,
 ):
     own = own_place()
@@ -168,12 +168,15 @@
         pltpu.make_async_copy(in_len_hbm, in_len, load_sem.at[7]),
         pltpu.make_async_copy(res_len_hbm, res_len, load_sem.at[8]),
     ]
-    for load in loads:
+    early, late = loads[:3] + loads[6:], loads[3:6]
+    for load in early:
         load.start()
     barrier = pltpu.get_barrier_semaphore()
     for offset in OFFSETS:
         pl.semaphore_signal(barrier, inc=1, device_id=place_at(own, offset), device_id_type=MESH)
-    for load in loads[:3] + loads[6:]:
+    for load in late:
+        load.start()
+    for load in early:
         load.wait()
     same_group = lax.broadcasted_iota(jnp.int32, (N_SEQ, N_SEQ), 0) == lax.broadcasted_iota(
         jnp.int32, (N_SEQ, N_SEQ), 1
@@ -197,7 +200,7 @@
                 column, (N_SEQ, HEAD_SIZE)
             )
 
-        @pl.loop(0, N_SEQ)
+        @pl.loop(0, N_SEQ, unroll=2)
         def _(group):
             rows = anchor_rows[pl.ds(group, 1), :] + scale_rows[pl.ds(group, 1), :] * delta[
                 request, group
@@ -206,17 +209,6 @@
                 jnp.bfloat16
             )
 
-    for load in loads[3:5]:
-        load.wait()
-    read_cards(queries, fresh, cards)
-    for source in range(N_SRC):
-        place = jnp.int32(0)
-        for local in range(4):
-            slot = assign[source * 4 + local] - src * 4
-            place = jnp.where(jnp.logical_and(slot >= 0, slot < 4), slot, place)
-        cards_out[source] = cards[place]
-    cards_in[src] = cards_out[src]
-
     mine = src * N_SEQ + seq
     keep = pltpu.make_async_copy(
         rebuilt.at[src, pl.ds(pl.multiple_of(seq * GROUP, GROUP), GROUP), :],
@@ -225,17 +217,6 @@
     )
     keep.start()
     pl.semaphore_wait(barrier, len(OFFSETS))
-
-    card_copies = []
-    for turn in range(1, N_SRC):
-        to_src = lax.rem(src + turn, N_SRC)
-        card_copies.append(
-            remote(
-                cards_out.at[to_src], cards_in.at[src],
-                card_send.at[turn - 1], card_recv.at[turn - 1], (to_src, seq),
-            )
-        )
-        card_copies[-1].start()
 
     copies = []
     work = [(half, offset) for half in range(2) for offset in OFFSETS]
@@ -257,11 +238,64 @@
             copy.start()
             copies.append(copy)
 
-    pump(WINDOW)
+    pump(PUMP_FIRST)
+    for load in late[:2]:
+        load.wait()
+    read_cards(queries, fresh, cards, news)
+    for source in range(N_SRC):
+        place = jnp.int32(0)
+        for local in range(4):
+            slot = assign[source * 4 + local] - src * 4
+            place = jnp.where(jnp.logical_and(slot >= 0, slot < 4), slot, place)
+        cards_out[source] = cards[place]
+        news_out[source] = news[place]
+    cards_in[src] = cards_out[src]
+    news_in[src] = news_out[src]
+    half = pl.ds(pl.multiple_of(core * (QUERY_ROWS // 2), QUERY_ROWS // 2), QUERY_ROWS // 2)
+    card_copies, new_copies, swap_copies = [], [], []
+    for turn in range(1, N_SRC):
+        to_src = lax.rem(src + turn, N_SRC)
+        from_src = lax.rem(src + N_SRC - turn, N_SRC)
+        card_copies.append(
+            remote(
+                cards_out.at[to_src, half], cards_in.at[src, half],
+                card_send.at[turn - 1], card_recv.at[turn - 1], (to_src, seq),
+            )
+        )
+        new_copies.append(
+            remote(
+                news_out.at[to_src], news_in.at[src],
+                new_send.at[turn - 1], new_recv.at[turn - 1], (to_src, seq),
+            )
+        )
+        swap_copies.append(
+            remote(
+                cards_in.at[from_src, half], cards_in.at[from_src, half],
+                swap_send.at[turn - 1], swap_recv.at[turn - 1], sibling,
+            )
+        )
     for copy in card_copies:
-        copy.wait()
-    loads[5].wait()
-
+        copy.start()
+
+    @pl.when(seq == 0)
+    def _():
+        for copy in new_copies:
+            copy.start()
+
+    pump(WINDOW - PUMP_FIRST)
+    for copy, swap in zip(card_copies, swap_copies):
+        copy.wait_recv()
+        swap.start()
+    for copy, swap in zip(card_copies, swap_copies):
+        copy.wait_send()
+        swap.wait()
+
+    @pl.when(seq == 0)
+    def _():
+        for copy in new_copies:
+            copy.wait()
+
+    late[2].wait()
     first = seq == 0
     ahead = lax.broadcasted_iota(jnp.int32, (1, SPAN), 1)
     in_position = ahead // GROUP * SPAN + seq * GROUP + ahead % GROUP
@@ -273,16 +307,16 @@
         res_live = res_position < res_len[src * 4 + block]
         for start in (0, 4):
 
-            @pl.loop(start, start + 4)
+            @pl.loop(start, start + 4, unroll=2)
             def _(head):
                 keys = pl.ds(pl.multiple_of(head * HEAD_SIZE, HEAD_SIZE), HEAD_SIZE)
                 values = pl.ds(pl.multiple_of(KEY_WIDTH + head * HEAD_SIZE, HEAD_SIZE), HEAD_SIZE)
                 in_peak, in_total, in_sum = partial_of(
-                    cards_in.at[block], rebuilt[block, :, keys], rebuilt[block, :, values],
+                    cards_in.at[block], news_in.at[block], rebuilt[block, :, keys], rebuilt[block, :, values],
                     in_live, first, head,
                 )
                 res_peak, res_total, res_sum = partial_of(
-                    cards.at[4 + block], resident[block, :, keys], resident[block, :, values],
+                    cards.at[4 + block], news.at[4 + block], resident[block, :, keys], resident[block, :, values],
                     res_live, first, head,
                 )
                 to_core, to_plane = head % 2, block * 4 + head // 2
@@ -322,7 +356,7 @@
     stat_lane = lax.broadcasted_iota(jnp.int32, (1, HEAD_SIZE), 1)
     is_peak = stat_lane % 64 < 32
 
-    @pl.loop(0, PLANE)
+    @pl.loop(0, PLANE, unroll=4)
     def _(pair):
         here, there = stat_out[core, pair], core_stat[pair]
         peak = jnp.maximum(here, there)
@@ -364,7 +398,7 @@
         )
 
     zero = jnp.zeros((ROWS, HEAD_SIZE), jnp.float32)
-    sums = lax.fori_loop(0, PLANE, add, (zero, zero))
+    sums = lax.fori_loop(0, PLANE, add, (zero, zero), unroll=4)
     for kind in range(2):
         result[kind] = sums[kind].astype(jnp.bfloat16)
 
@@ -395,7 +429,9 @@
         ).start()
     keep.wait()
     at_home.start()
-    pump(PUMP_RESULT)
+    pump(len(work))
+    for copy in copies[-WINDOW:]:
+        copy.wait_send()
     at_home.wait()
     take_bytes(result_out.at[0, core], result_recv.at[0])
     take_bytes(result_out.at[1, core, others], result_recv.at[1])
@@ -408,15 +444,12 @@
     ]
     for copy in back_copies:
         copy.start()
-    pump(len(work))
     take_bytes(stat_in.at[others], pair_send.at[0])
     take_bytes(part_in.at[others], pair_send.at[1])
     take_bytes(result_out.at[0, core], result_send.at[0])
     take_bytes(result_out.at[1, core, others], result_send.at[1])
     for copy in back_copies:
         copy.wait()
-    for copy in copies[-WINDOW:]:
-        copy.wait_send()
     take_bytes(recv_hbm.at[pl.ds(0, len(OFFSETS))], recv_sem)
 
 
@@ -445,12 +478,15 @@
             pltpu.VMEM(resident.shape, bf16),
             pltpu.VMEM(queries.shape, bf16),
             pltpu.VMEM(fresh.shape, bf16),
-            pltpu.VMEM((8, CARD, HEAD_SIZE), bf16),
+            pltpu.VMEM((8, QUERY_ROWS, HEAD_SIZE), bf16),
+            pltpu.VMEM((8, NEW_ROWS, HEAD_SIZE), bf16),
             pltpu.VMEM((N_SEQ, FEAT), f32),
             pltpu.VMEM((N_SEQ, FEAT), f32),
             pltpu.VMEM((N_SRC, SPAN, FEAT), bf16),
-            pltpu.VMEM((N_SRC, CARD, HEAD_SIZE), bf16),
-            pltpu.VMEM((N_SRC, CARD, HEAD_SIZE), bf16),
+            pltpu.VMEM((N_SRC, QUERY_ROWS, HEAD_SIZE), bf16),
+            pltpu.VMEM((N_SRC, QUERY_ROWS, HEAD_SIZE), bf16),
+            pltpu.VMEM((N_SRC, NEW_ROWS, HEAD_SIZE), bf16),
+            pltpu.VMEM((N_SRC, NEW_ROWS, HEAD_SIZE), bf16),
             pltpu.VMEM((2, PLANE, 2, ROWS, HEAD_SIZE), bf16),
             pltpu.VMEM((2, PLANE, 1, HEAD_SIZE), f32),
             pltpu.VMEM((PLANE, 2, ROWS, HEAD_SIZE), bf16),
@@ -468,6 +504,10 @@
             pltpu.SemaphoreType.DMA,
             pltpu.SemaphoreType.DMA((3,)),
             pltpu.SemaphoreType.DMA((3,)),
+            pltpu.SemaphoreType.DMA((3,)),
+            pltpu.SemaphoreType.DMA((3,)),
+            pltpu.SemaphoreType.DMA((3,)),
+            pltpu.SemaphoreType.DMA((3,)),
             pltpu.SemaphoreType.DMA((2,)),
             pltpu.SemaphoreType.DMA((2,)),
             pltpu.SemaphoreType.DMA((2,)),
@@ -487,19 +527,20 @@
 
 
 def place_kernel(
-    assign_hbm, in_len_hbm, recv, result, in_cache, attention,
-    assign, in_len, zeros, edge, out_sem, edge_sem, load_sem,
+    assign_hbm, in_len_hbm, recv, result_ref, in_cache, attention,
+    assign, in_len, result, unpacked, zeros, edge, out_sem, edge_sem, load_sem,
 ):
     src, seq = lax.axis_index("src"), lax.axis_index("seq")
     loads = [
         pltpu.make_async_copy(assign_hbm, assign, load_sem.at[0]),
         pltpu.make_async_copy(in_len_hbm, in_len, load_sem.at[1]),
+        pltpu.make_async_copy(result_ref, result, load_sem.at[2]),
     ]
     for load in loads:
         load.start()
-    for load in loads:
+    zeros[...] = jnp.zeros_like(zeros)
+    for load in loads[:2]:
         load.wait()
-    zeros[...] = jnp.zeros_like(zeros)
     sources, counts = [], []
     for slot in range(4):
         source, length = jnp.int32(0), jnp.int32(0)
@@ -512,22 +553,31 @@
         counts.append(count)
         whole = count // EDGE
         cut = whole * EDGE < count
-        for part in range(SPAN // EDGE):
-            rows = pl.ds(part * EDGE, EDGE)
-
-            @pl.when(part < whole)
-            def _():
-                pltpu.make_async_copy(
-                    recv.at[source, rows], in_cache.at[slot, rows], out_sem
-                ).start()
-
-            @pl.when(jnp.logical_and(part == whole, cut))
-            def _():
-                pltpu.make_async_copy(recv.at[source, rows], edge.at[slot], edge_sem.at[slot]).start()
-
-            @pl.when(jnp.logical_and(part >= whole, jnp.logical_or(part > whole, ~cut)))
-            def _():
-                pltpu.make_async_copy(zeros, in_cache.at[slot, rows], out_sem).start()
+
+        @pl.when(whole == SPAN // EDGE)
+        def _():
+            pltpu.make_async_copy(recv.at[source], in_cache.at[slot], out_sem).start()
+
+        @pl.when(whole < SPAN // EDGE)
+        def _():
+            for part in range(SPAN // EDGE):
+                rows = pl.ds(part * EDGE, EDGE)
+
+                @pl.when(part < whole)
+                def _():
+                    pltpu.make_async_copy(
+                        recv.at[source, rows], in_cache.at[slot, rows], out_sem
+                    ).start()
+
+                @pl.when(jnp.logical_and(part == whole, cut))
+                def _():
+                    pltpu.make_async_copy(
+                        recv.at[source, rows], edge.at[slot], edge_sem.at[slot]
+                    ).start()
+
+                @pl.when(jnp.logical_and(part >= whole, jnp.logical_or(part > whole, ~cut)))
+                def _():
+                    pltpu.make_async_copy(zeros, in_cache.at[slot, rows], out_sem).start()
 
     row = lax.broadcasted_iota(jnp.int32, (EDGE, FEAT), 0)
     for slot in range(4):
@@ -541,38 +591,43 @@
             rows = pl.ds(pl.multiple_of(whole * EDGE, EDGE), EDGE)
             pltpu.make_async_copy(edge.at[slot], in_cache.at[slot, rows], out_sem).start()
 
+    loads[2].wait()
     for slot in range(8):
         for head in range(KEY_VALUE_HEADS):
             first = sources[slot] if slot < 4 else slot - 4
             rows = result[slot // 4, head % 2, first * 4 + head // 2].astype(jnp.float32)
             for column in range(8):
                 low = (head * 8 + column) * HEAD_SIZE
-                attention[slot, :, low : low + HEAD_SIZE] = rows[
+                unpacked[slot, :, low : low + HEAD_SIZE] = rows[
                     column * 4 : column * 4 + 4, :
                 ].astype(jnp.bfloat16)
+    last = pltpu.make_async_copy(unpacked, attention, load_sem.at[3])
+    last.start()
+    last.wait()
     pltpu.make_async_copy(in_cache, in_cache, out_sem).wait()
 
 
 def place(assign, in_len, recv, result):
-    scalars = pl.BlockSpec(memory_space=pltpu.HBM)
-    whole = pl.BlockSpec(memory_space=pltpu.VMEM)
     any_space = pl.BlockSpec(memory_space=pl.ANY)
+    attention = (8, 4, QUERY_HEADS * HEAD_SIZE)
     return pl.pallas_call(
         place_kernel,
         out_shape=(
-            jax.ShapeDtypeStruct((4, SPAN, FEAT), jnp.bfloat16),
-            jax.ShapeDtypeStruct((8, 4, QUERY_HEADS * HEAD_SIZE), jnp.bfloat16),
+            pltpu.HBM((4, SPAN, FEAT), jnp.bfloat16),
+            pltpu.HBM(attention, jnp.bfloat16),
         ),
-        in_specs=[scalars, scalars, any_space, whole],
-        out_specs=(any_space, whole),
+        in_specs=[any_space] * 4,
+        out_specs=(any_space, any_space),
         scratch_shapes=[
             pltpu.SMEM((16,), jnp.int32),
             pltpu.SMEM((16,), jnp.int32),
+            pltpu.VMEM(result.shape, jnp.bfloat16),
+            pltpu.VMEM(attention, jnp.bfloat16),
             pltpu.VMEM((EDGE, FEAT), jnp.bfloat16),
             pltpu.VMEM((4, EDGE, FEAT), jnp.bfloat16),
             pltpu.SemaphoreType.DMA,
             pltpu.SemaphoreType.DMA((4,)),
-            pltpu.SemaphoreType.DMA((2,)),
+            pltpu.SemaphoreType.DMA((4,)),
         ],
         compiler_params=pltpu.CompilerParams(vmem_limit_bytes=16 * MIB),
     )(

time: 127 us -> 122 us (0.961)
  Pallas kernels: 126 us -> 121 us
    pallas_call x1, Pallas kernels: 121 us -> 117 us  [move(): pl.pallas_call(move_kernel, out_shape=(pltpu.VMEM((N_SRC * N_SEQ, GROUP,...]
where the time goes in v3:
time: 122 us
  Pallas kernels  121 us (99%)
    pallas_call x1, Pallas kernels, move(): pl.pallas_call(move_kernel, out_shape=(pltpu.VMEM((N_SRC * N_SEQ, GROUP,...  117 us
    pallas_call x1, Pallas kernels, place(): pl.pallas_call(place_kernel, out_shape=(pltpu.HBM((4, SPAN, FEAT), jnp.bf...  4.22 us

profile of v3, /device:TPU:1, one launch (start us, length us, event | category | flops | bytes accessed | tf_op | source)
XLA Modules:
  0.0 121.7 jit_solution(9071490610473855270)
XLA Ops:
  0.6 116.8 %shard_map.104 = (bf16[128,16,2048]{2,1,0:T(8,128)(2,1)S(1)}, bf16[2,2,16,32,128]{4,3,2,1,0:T(8,128)(2,1)S(1)}) custom-call(s32[16]{0:T(128)} %assign_hbm.3, s32[16]{0:T(128)} %in_len_hbm.3, s32[16]{0:T(128)} %res_len_hbm.1, bf16[4,32,16,2048]{3,2,1,0:T(8,128)(2,1)} %bitcast.7, bf16[4,32,2048]{2,1,0:T(8,128)(2,1)} %bitcast.8, f32[4,16,32]{2,1,0:T(8,128)} %bitcast.9, ...), custom_call_target="tpu_custom_call" | custom-call | tf_op jit(solution)/shard_map/pallas_call | solution.py:463
  117.5 4.2 %shard_map.105 = (bf16[4,512,2048]{2,1,0:T(8,128)(2,1)}, bf16[8,4,8192]{2,1,0:T(4,128)(2,1)}) custom-call(s32[16]{0:T(128)} %assign_hbm.3, s32[16]{0:T(128)} %in_len_hbm.3, bf16[4,512,2048]{2,1,0:T(8,128)(2,1)S(1)} %bitcast.6, bf16[2,2,16,32,128]{4,3,2,1,0:T(8,128)(2,1)S(1)} %get-tuple-element.5.result_ref), custom_call_target="tpu_custom_call" | custom-call | tf_op jit(solution)/shard_map/pallas_call | solution.py:613

commit v4 on v3

--- a/solution.py
+++ b/solution.py
@@ -169,12 +169,11 @@
         pltpu.make_async_copy(res_len_hbm, res_len, load_sem.at[8]),
     ]
     early, late = loads[:3] + loads[6:], loads[3:6]
-    for load in early:
-        load.start()
+    loads[2].start()
     barrier = pltpu.get_barrier_semaphore()
     for offset in OFFSETS:
         pl.semaphore_signal(barrier, inc=1, device_id=place_at(own, offset), device_id_type=MESH)
-    for load in late:
+    for load in loads[:2] + loads[6:] + late:
         load.start()
     for load in early:
         load.wait()
@@ -556,7 +555,11 @@
 
         @pl.when(whole == SPAN // EDGE)
         def _():
-            pltpu.make_async_copy(recv.at[source], in_cache.at[slot], out_sem).start()
+            for part in range(4):
+                rows = pl.ds(part * (SPAN // 4), SPAN // 4)
+                pltpu.make_async_copy(
+                    recv.at[source, rows], in_cache.at[slot, rows], out_sem
+                ).start()
 
         @pl.when(whole < SPAN // EDGE)
         def _():

time: 122 us -> 122 us (level)
  no operation moved by 1% of the time
where the time goes in v4:
time: 122 us
  Pallas kernels  121 us (99%)
    pallas_call x1, Pallas kernels, move(): pl.pallas_call(move_kernel, out_shape=(pltpu.VMEM((N_SRC * N_SEQ, GROUP,...  117 us
    pallas_call x1, Pallas kernels, place(): pl.pallas_call(place_kernel, out_shape=(pltpu.HBM((4, SPAN, FEAT), jnp.bf...  4.21 us

profile of v4, /device:TPU:1, one launch (start us, length us, event | category | flops | bytes accessed | tf_op | source)
XLA Modules:
  0.0 121.8 jit_solution(16690282610251862453)
XLA Ops:
  0.6 116.9 %shard_map.104 = (bf16[128,16,2048]{2,1,0:T(8,128)(2,1)S(1)}, bf16[2,2,16,32,128]{4,3,2,1,0:T(8,128)(2,1)S(1)}) custom-call(s32[16]{0:T(128)} %assign_hbm.3, s32[16]{0:T(128)} %in_len_hbm.3, s32[16]{0:T(128)} %res_len_hbm.1, bf16[4,32,16,2048]{3,2,1,0:T(8,128)(2,1)} %bitcast.7, bf16[4,32,2048]{2,1,0:T(8,128)(2,1)} %bitcast.8, f32[4,16,32]{2,1,0:T(8,128)} %bitcast.9, ...), custom_call_target="tpu_custom_call" | custom-call | tf_op jit(solution)/shard_map/pallas_call | solution.py:462
  117.6 4.2 %shard_map.105 = (bf16[4,512,2048]{2,1,0:T(8,128)(2,1)}, bf16[8,4,8192]{2,1,0:T(4,128)(2,1)}) custom-call(s32[16]{0:T(128)} %assign_hbm.3, s32[16]{0:T(128)} %in_len_hbm.3, bf16[4,512,2048]{2,1,0:T(8,128)(2,1)S(1)} %bitcast.6, bf16[2,2,16,32,128]{4,3,2,1,0:T(8,128)(2,1)S(1)} %get-tuple-element.5.result_ref), custom_call_target="tpu_custom_call" | custom-call | tf_op jit(solution)/shard_map/pallas_call | solution.py:616
